TPU v7x, 512 devices: a whole 4x4x16 slice. The times are simulated.
512 devices in a mesh: expert: 128 (over z, y, core), token: 4 (over x).
Axes of the slice: x: 4, y: 4, z: 16, core: 2. Of those that a mesh axis runs over, the one named last changes fastest.
Arguments:
- tokens: bfloat16 [8192, 2048], P(('expert', 'token')), may hold values from -6 to 6
- routes: int32 [8192, 8], P(('expert', 'token')), may hold values from 0 to 127, all different within a row; in each aligned block of 16 rows (0 to 15, 16 to 31, ...) at most 2 rows name the same one
- assign: int32 [128], replicated, may hold values from 0 to 31, as said below
- gate_weight: bfloat16 [128, 2048, 1536], P('expert', None, 'token'), may hold values from -0.125 to 0.125
- up_weight: bfloat16 [128, 2048, 1536], P('expert', None, 'token'), may hold values from -0.125 to 0.125
- sketch: bfloat16 [128, 1536, 512], P('expert', 'token'), may hold values from -6 to 6
Outputs:
- hidden: bfloat16 [128, 1024, 1536], P('expert', None, 'token')
Inputs may be any that keep to these rules, and one draw needn't show every extreme that they name: `routes`: within each aligned block of 16 tokens each token names 8 different experts, and no expert is named by more than 2 entries of the block. `assign`: every one of the 32 clusters has at least two experts.
All inputs are finite; a program needn't handle non-finite values.
Results may differ from a plain program's by a relative error of at most 0.029.
Values may be sent and summed in bfloat16 or wider, within the bound.
A program may use at most 64 MiB of HBM per device.

v0:
```python
import jax
import jax.numpy as jnp
from jax import lax
from jax.sharding import PartitionSpec as P


def place_tokens(tok_rows, tok_ids, expert_count, capacity):
    flat_ids = tok_ids.reshape(-1)
    expert_hits = (flat_ids[:, None] == jnp.arange(expert_count, dtype=jnp.int32)[None, :]).astype(
        jnp.int32
    )
    earlier = jnp.cumsum(expert_hits, axis=0) - expert_hits
    slot_index = jnp.sum(earlier * expert_hits, axis=1)
    target = flat_ids * capacity + slot_index
    select = (
        jnp.arange(expert_count * capacity, dtype=jnp.int32)[:, None] == target[None, :]
    ).astype(jnp.float32)
    select = (
        select.reshape(expert_count * capacity, tok_rows.shape[0], tok_ids.shape[1])
        .sum(axis=2)
        .astype(jnp.bfloat16)
    )
    filled = jnp.dot(select, tok_rows, preferred_element_type=jnp.float32).astype(jnp.bfloat16)
    return filled.reshape(expert_count, capacity, tok_rows.shape[1])


def new_basis(partial_term, member, assign, token_count, expert_count):
    rank_cols = partial_term.shape[1]
    row_block = partial_term.shape[0] // (token_count * expert_count)
    pieces = partial_term.reshape(token_count, expert_count * row_block, rank_cols)
    arrived = lax.all_to_all(pieces, "expert", split_axis=1, concat_axis=1, tiled=True)
    arrived = arrived.reshape(token_count, expert_count, row_block, rank_cols)
    by_cluster = jnp.einsum("ci,tirk->ctrk", member, arrived, preferred_element_type=jnp.float32)
    own_rows = lax.psum_scatter(
        by_cluster.astype(jnp.bfloat16), "token", scatter_dimension=1, tiled=True
    ).astype(jnp.float32)
    outgoing = jnp.take(own_rows[:, 0], assign, axis=0).astype(jnp.bfloat16)
    returned = lax.all_to_all(outgoing, "expert", split_axis=0, concat_axis=0, tiled=True)
    cluster_rows = returned.reshape(expert_count * row_block, rank_cols)
    local_gram = lax.dot_general(
        cluster_rows, cluster_rows, (((0,), (0,)), ((), ())), preferred_element_type=jnp.float32
    )
    column_gram = lax.psum(local_gram.astype(jnp.bfloat16), "token").astype(jnp.float32)
    lower_factor = jnp.linalg.cholesky(column_gram)
    solved = jax.scipy.linalg.solve_triangular(
        lower_factor, cluster_rows.astype(jnp.float32).T, lower=True
    )
    basis_part = solved.T.astype(jnp.bfloat16)
    return lax.all_gather(basis_part, "token", axis=0, tiled=True)


def per_device(tokens, routes, assign, gate_weight, up_weight, sketch):
    expert_count = lax.axis_size("expert")
    token_count = lax.axis_size("token")
    cluster_count = expert_count // 4
    gate_local = gate_weight[0]
    up_local = up_weight[0]
    member = (assign[None, :] == jnp.arange(cluster_count, dtype=jnp.int32)[:, None]).astype(
        jnp.bfloat16
    )
    partial_term = jnp.dot(up_local, sketch[0], preferred_element_type=jnp.float32).astype(
        jnp.bfloat16
    )
    basis = new_basis(partial_term, member, assign, token_count, expert_count)
    projected = lax.dot_general(
        up_local, basis, (((0,), (0,)), ((), ())), preferred_element_type=jnp.float32
    ).astype(jnp.bfloat16)
    partial_term = jnp.dot(up_local, projected, preferred_element_type=jnp.float32).astype(
        jnp.bfloat16
    )
    basis = new_basis(partial_term, member, assign, token_count, expert_count)
    shard_rows = tokens.shape[0]
    capacity = max(2, 2 * shard_rows * routes.shape[1] // expert_count)
    outgoing = place_tokens(tokens, routes, expert_count, capacity)
    arrived = lax.all_to_all(outgoing, "expert", split_axis=0, concat_axis=0, tiled=True)
    slots_in = lax.all_gather(arrived, "token", axis=0, tiled=True)
    slots_in = slots_in.reshape(-1, tokens.shape[1])
    gate_value = jnp.dot(slots_in, gate_local, preferred_element_type=jnp.float32)
    on_basis = jnp.dot(slots_in, basis, preferred_element_type=jnp.float32).astype(jnp.bfloat16)
    coefficient = lax.dot_general(
        basis, up_local, (((0,), (0,)), ((), ())), preferred_element_type=jnp.float32
    ).astype(jnp.bfloat16)
    merged = jnp.dot(on_basis, coefficient, preferred_element_type=jnp.float32)
    hidden = (jax.nn.silu(gate_value) * merged).astype(jnp.bfloat16)
    return hidden[None]


def solution(mesh):
    return jax.shard_map(
        per_device,
        mesh=mesh,
        in_specs=(
            P(("expert", "token"), None),
            P(("expert", "token"), None),
            P(),
            P("expert", None, "token"),
            P("expert", None, "token"),
            P("expert", "token", None),
        ),
        out_specs=P("expert", None, "token"),
        check_vma=False,
    )
```

profile of v0, /device:TPU:1, one launch (start us, length us, event | category | flops | bytes accessed | tf_op | source)
XLA Modules:
  0.0 931.0 jit_solution(862876491536003445)
XLA Ops:
  11.8 117.2 %all_to_all.25 = bf16[4,512,512]{2,0,1:T(4,128)(2,1)S(1)} all-to-all(bf16[4,512,512]{2,0,1:T(4,128)(2,1)S(1)} %copy.53), channel_id=1, replica_groups=mesh['expert'=128,'token'=4] {'expert'}, dimensions={1} | all-to-all | bytes 4194304 | tf_op jit(solution)/shard_map/all_to_all | solution.py:31
  132.4 22.3 %reduce-scatter.3.cloned.1.call-done = bf16[32,1,4,512]{3,0,2,1:T(8,128)(2,1)} async-done(((bf16[32,4,4,512]{3,0,2,1:T(8,128)(2,1)}), bf16[32,1,4,512]{3,0,2,1:T(8,128)(2,1)}) %reduce-scatter.3.cloned.1.call-update) | async-done | bytes 131088 | tf_op jit(solution)/shard_map/reduce_scatter | solution.py:34
  157.0 48.9 %all_to_all.26 = bf16[128,4,512]{2,1,0:T(4,128)(2,1)S(1)} all-to-all(bf16[128,4,512]{2,1,0:T(4,128)(2,1)S(1)} %select_convert_fusion.1), channel_id=1, replica_groups=mesh['expert'=128,'token'=4] {'expert'}, dimensions={0} | all-to-all | bytes 1048576 | tf_op jit(solution)/shard_map/all_to_all | solution.py:38
  208.9 47.0 %all-reduce.4.cloned.1.call-done = bf16[512,512]{0,1:T(8,128)(2,1)} async-done(((bf16[512,512]{0,1:T(8,128)(2,1)}), bf16[512,512]{0,1:T(8,128)(2,1)}) %all-reduce.4.cloned.1.call-update) | async-done | bytes 524304 | tf_op jit(solution)/shard_map/psum | solution.py:43
  259.4 11.7 %cholesky.286 = f32[128,128]{1,0:T(8,128)S(1)} custom-call(f32[128,128]{1,0:T(8,128)S(1)} %cholesky.426), custom_call_target="Cholesky" | custom-call | tf_op jit(solution)/shard_map/jit(cholesky)/cholesky | solution.py:44
  283.6 11.7 %cholesky.305 = f32[128,128]{1,0:T(8,128)S(1)} custom-call(f32[128,128]{1,0:T(8,128)S(1)} %cholesky.430), custom_call_target="Cholesky" | custom-call | tf_op jit(solution)/shard_map/jit(cholesky)/cholesky | solution.py:44
  307.0 11.7 %cholesky.326 = f32[128,128]{1,0:T(8,128)S(1)} custom-call(f32[128,128]{1,0:T(8,128)S(1)} %cholesky.435), custom_call_target="Cholesky" | custom-call | tf_op jit(solution)/shard_map/jit(cholesky)/cholesky | solution.py:44
  330.6 11.7 %cholesky.343 = f32[128,128]{1,0:T(8,128)S(1)} custom-call(f32[128,128]{1,0:T(8,128)S(1)} %convolution_subtract_fusion.11), custom_call_target="Cholesky" | custom-call | tf_op jit(solution)/shard_map/jit(cholesky)/cholesky | solution.py:44
  347.8 11.5 %while.4 = (s32[]{:T(128)}, f32[512,512]{1,0:T(8,128)}, s32[4,2]{0,1:T(2,128)S(1)}, f32[4,128,128]{2,1,0:T(8,128)S(1)}, s32[]{:T(128)}) while((s32[]{:T(128)}, f32[512,512]{1,0:T(8,128)}, s32[4,2]{0,1:T(2,128)S(1)}, f32[4,128,128]{2,1,0:T(8,128)S(1)}, s32[]{:T(128)}) %tuple.52), condition=%wide.while_cond, body=%wide.while_body.sunk | while | flops 2 | bytes 131189 | solution.py:45
  359.4 39.3 %custom-call.30 = f32[4,128,128]{1,2,0:T(8,128)S(1)} custom-call(f32[4,128,128]{2,1,0:T(8,128)S(1)} %get-tuple-element.22), custom_call_target="InvertDiagBlocksLowerTriangular" | custom-call | tf_op jit(solution)/shard_map/jit(_solve_triangular)/triangular_solve | solution.py:45
  406.6 41.5 %all-gather.6.cloned.1.call-done = bf16[2048,512]{0,1:T(8,128)(2,1)} async-done(((bf16[512,512]{0,1:T(8,128)(2,1)}), bf16[2048,512]{0,1:T(8,128)(2,1)}) %all-gather.6.cloned.1.call-update) | async-done | bytes 2097168 | tf_op jit(solution)/shard_map/all_gather | solution.py:49
  464.3 113.7 %all_to_all.27 = bf16[4,512,512]{2,0,1:T(4,128)(2,1)S(1)} all-to-all(bf16[4,512,512]{2,0,1:T(4,128)(2,1)} %copy.61), channel_id=1, replica_groups=mesh['expert'=128,'token'=4] {'expert'}, dimensions={1} | all-to-all | bytes 4194304 | tf_op jit(solution)/shard_map/all_to_all | solution.py:31
  581.2 21.1 %reduce-scatter.5.cloned.1.call-done = bf16[32,1,4,512]{3,0,2,1:T(8,128)(2,1)} async-done(((bf16[32,4,4,512]{3,0,2,1:T(8,128)(2,1)}), bf16[32,1,4,512]{3,0,2,1:T(8,128)(2,1)}) %reduce-scatter.5.cloned.1.call-update) | async-done | bytes 131088 | tf_op jit(solution)/shard_map/reduce_scatter | solution.py:34
  605.5 18.3 %all-to-all-start.4 = ((bf16[128,4,512]{2,1,0:T(4,128)(2,1)}), bf16[128,4,512]{2,1,0:T(4,128)(2,1)S(1)}, u32[]{:S(2)}, u32[]{:S(2)}) async-start(bf16[128,4,512]{2,1,0:T(4,128)(2,1)} %select_convert_fusion), calls=%async_computation.6 | async-start | bytes 1048576 | tf_op jit(solution)/shard_map/all_to_all | solution.py:38
  626.6 28.0 %all-to-all-done.4 = bf16[128,4,512]{2,1,0:T(4,128)(2,1)S(1)} async-done(((bf16[128,4,512]{2,1,0:T(4,128)(2,1)}), bf16[128,4,512]{2,1,0:T(4,128)(2,1)S(1)}, u32[]{:S(2)}, u32[]{:S(2)}) %all-to-all-start.4) | async-done | bytes 524320 | tf_op jit(solution)/shard_map/all_to_all | solution.py:38
  665.1 50.4 %all-to-all-done = bf16[128,2,2048]{2,1,0:T(2,128)(2,1)S(1)} async-done(((bf16[128,2,2048]{2,1,0:T(2,128)(2,1)}), bf16[128,2,2048]{2,1,0:T(2,128)(2,1)S(1)}, u32[]{:S(2)}, u32[]{:S(2)}) %all-to-all-start) | async-done | bytes 1048608 | tf_op jit(solution)/shard_map/all_to_all | solution.py:75
  725.7 11.7 %cholesky.358 = f32[128,128]{1,0:T(8,128)S(1)} custom-call(f32[128,128]{1,0:T(8,128)S(1)} %cholesky.439), custom_call_target="Cholesky" | custom-call | tf_op jit(solution)/shard_map/jit(cholesky)/cholesky | solution.py:44
  749.9 11.7 %cholesky.377 = f32[128,128]{1,0:T(8,128)S(1)} custom-call(f32[128,128]{1,0:T(8,128)S(1)} %cholesky.443), custom_call_target="Cholesky" | custom-call | tf_op jit(solution)/shard_map/jit(cholesky)/cholesky | solution.py:44
  761.7 10.2 %custom-call.32 = f32[1,128,128]{1,2,0:T(8,128)S(1)} custom-call(f32[1,128,128]{2,1,0:T(8,128)S(1)} %get-tuple-element.50), custom_call_target="InvertDiagBlocksLowerTriangular" | custom-call | tf_op jit(solution)/shard_map/jit(cholesky)/cholesky | solution.py:44
  773.4 11.7 %cholesky.398 = f32[128,128]{1,0:T(8,128)S(1)} custom-call(f32[128,128]{1,0:T(8,128)S(1)} %cholesky.448), custom_call_target="Cholesky" | custom-call | tf_op jit(solution)/shard_map/jit(cholesky)/cholesky | solution.py:44
  796.4 11.7 %cholesky.415 = f32[128,128]{1,0:T(8,128)S(1)} custom-call(f32[128,128]{1,0:T(8,128)S(1)} %convolution_subtract_fusion.10), custom_call_target="Cholesky" | custom-call | tf_op jit(solution)/shard_map/jit(cholesky)/cholesky | solution.py:44
  814.6 11.3 %while.5 = (s32[]{:T(128)}, f32[512,512]{1,0:T(8,128)}, s32[4,2]{0,1:T(2,128)S(1)}, f32[4,128,128]{2,1,0:T(8,128)S(1)}, s32[]{:T(128)}) while((s32[]{:T(128)}, f32[512,512]{1,0:T(8,128)}, s32[4,2]{0,1:T(2,128)S(1)}, f32[4,128,128]{2,1,0:T(8,128)S(1)}, s32[]{:T(128)}) %tuple.72), condition=%wide.while_cond.clone, body=%wide.while_body.clone.sunk | while | flops 2 | bytes 131189 | solution.py:45
  825.9 39.3 %custom-call.34 = f32[4,128,128]{1,2,0:T(8,128)S(1)} custom-call(f32[4,128,128]{2,1,0:T(8,128)S(1)} %get-tuple-element.23), custom_call_target="InvertDiagBlocksLowerTriangular" | custom-call | tf_op jit(solution)/shard_map/jit(_solve_triangular)/triangular_solve | solution.py:45
  886.0 28.3 %all-gather.8.cloned.1.call-done = bf16[2048,512]{0,1:T(8,128)(2,1)} async-done(((bf16[512,512]{0,1:T(8,128)(2,1)}), bf16[2048,512]{0,1:T(8,128)(2,1)}) %all-gather.8.cloned.1.call-update) | async-done | bytes 2097168 | tf_op jit(solution)/shard_map/all_gather | solution.py:49
  (165 shorter events, 192.3 us)
Async XLA Ops:
  6.5 1.4 copy-start
  6.5 148.1 %reduce-scatter.3.cloned.1.call-start = ((), (), s32[]{:S(2)}) async-start(), calls=%async_computation.8 | async-start | bytes 655360 | tf_op jit(solution)/shard_map/reduce_scatter | solution.py:34
  11.8 117.2 %copy-start.8 = (s32[128]{0:T(128)S(1)}, s32[128]{0:T(128)}, u32[]{:S(2)}) copy-start(s32[128]{0:T(128)} %param.13) | copy-start | bytes 1540
  132.3 123.6 %all-reduce.4.cloned.1.call-start = ((), (), s32[]{:S(2)}) async-start(), calls=%async_computation.9 | async-start | bytes 1048576 | tf_op jit(solution)/shard_map/psum | solution.py:43
  207.3 240.7 %all-gather.6.cloned.1.call-start = ((), (), s32[]{:S(2)}) async-start(), calls=%async_computation.10 | async-start | bytes 2621440 | tf_op jit(solution)/shard_map/all_gather | solution.py:49
  258.4 1.0 copy-start.4
  347.8 54.0 %copy-start.2 = (f32[512,512]{0,1:T(8,128)S(1)}, f32[512,512]{0,1:T(8,128)}, u32[]{:S(2)}) copy-start(f32[512,512]{0,1:T(8,128)} %copy.60) | copy-start | bytes 3145732
  406.5 195.8 %reduce-scatter.5.cloned.1.call-start = ((), (), s32[]{:S(2)}) async-start(), calls=%async_computation.11 | async-start | bytes 655360 | tf_op jit(solution)/shard_map/reduce_scatter | solution.py:34
  581.2 42.6 %copy-start.7 = (s32[16,8]{0,1:T(8,128)S(1)}, s32[16,8]{0,1:T(8,128)}, u32[]{:S(2)}) copy-start(s32[16,8]{0,1:T(8,128)} %param.12) | copy-start | bytes 1540
  581.2 43.4 %copy-start.6 = (bf16[16,2048]{1,0:T(8,128)(2,1)S(1)}, bf16[16,2048]{1,0:T(8,128)(2,1)}, u32[]{:S(2)}) copy-start(bf16[16,2048]{1,0:T(8,128)(2,1)} %param.11) | copy-start | bytes 196612
  605.5 49.1 %all-to-all-start.4 = ((bf16[128,4,512]{2,1,0:T(4,128)(2,1)}), bf16[128,4,512]{2,1,0:T(4,128)(2,1)S(1)}, u32[]{:S(2)}, u32[]{:S(2)}) async-start(bf16[128,4,512]{2,1,0:T(4,128)(2,1)} %select_convert_fusion), calls=%async_computation.6 | async-start | bytes 1048576 | tf_op jit(solution)/shard_map/all_to_all | solution.py:38
  654.6 61.0 %all-to-all-start = ((bf16[128,2,2048]{2,1,0:T(2,128)(2,1)}), bf16[128,2,2048]{2,1,0:T(2,128)(2,1)S(1)}, u32[]{:S(2)}, u32[]{:S(2)}) async-start(bf16[128,2,2048]{2,1,0:T(2,128)(2,1)} %reshape.80), calls=%async_computation | async-start | bytes 2097152 | tf_op jit(solution)/shard_map/all_to_all | solution.py:75
  663.7 58.5 %all-reduce.6.cloned.1.call-start = ((), (), s32[]{:S(2)}) async-start(), calls=%async_computation.12 | async-start | bytes 1048576 | tf_op jit(solution)/shard_map/psum | solution.py:43
  665.1 208.0 %all-gather.4.cloned.1.call-start = ((), (), s32[]{:S(2)}) async-start(), calls=%async_computation.7 | async-start | bytes 5242880 | tf_op jit(solution)/shard_map/all_gather | solution.py:76
  715.5 1.0 copy-start.1
  716.5 197.8 %all-gather.8.cloned.1.call-start = ((), (), s32[]{:S(2)}) async-start(), calls=%async_computation.13 | async-start | bytes 2621440 | tf_op jit(solution)/shard_map/all_gather | solution.py:49
  724.7 1.0 copy-start.5
  814.5 53.8 %copy-start.3 = (f32[512,512]{0,1:T(8,128)S(1)}, f32[512,512]{0,1:T(8,128)}, u32[]{:S(2)}) copy-start(f32[512,512]{0,1:T(8,128)} %copy.68) | copy-start | bytes 3145732
  873.0 7.4 copy-start.9
  886.0 31.1 %copy-start.10 = (f32[1024,384]{1,0:T(8,128)S(1)}, f32[1024,384]{1,0:T(8,128)}, u32[]{:S(2)}) copy-start(f32[1024,384]{1,0:T(8,128)} %fusion.11) | copy-start | bytes 4718596
Sparse Core Ops, SparseCore 0:
  132.4 22.2 reduce-scatter.2
  207.4 48.4 all-reduce.3
  406.6 41.3 all-gather.5
  581.3 20.9 reduce-scatter.4
  666.6 55.6 all-reduce.5
  724.2 58.8 all-gather.3
  873.1 41.1 all-gather.7
where the time goes:
time: 940 us; the launch traced here: 931 us
  blocking collectives  280 us (30%)
  other arithmetic  246 us (26%)
  waiting for transfers between devices  243 us (26%)
  local copies, waits for them, and re-layouts  58.5 us (6%)
  matrix products  56.9 us (6%)
  starting transfers between devices  28 us (3%)
  between operations  19.3 us (2%)
    all_to_all x2, blocking collectives, new_basis(): lax.all_to_all(pieces, 'expert', split_axis=1, concat_axis=1, tiled=True)  231 us
    another operation x29, other arithmetic, new_basis(): lower_factor = jnp.linalg.cholesky(column_gram)  159 us
    another operation x5, other arithmetic, new_basis(): jax.scipy.linalg.solve_triangular(lower_factor, cluster_rows.astype(jnp.f...  80.9 us
    all_gather x2, waiting for transfers between devices, new_basis(): return lax.all_gather(basis_part, 'token', axis=0, tiled=True)  69.8 us
    psum x2, waiting for transfers between devices, new_basis(): lax.psum(local_gram.astype(jnp.bfloat16), 'token').astype(jnp.float32)  51 us
    all_to_all x1, waiting for transfers between devices, per_device(): lax.all_to_all(outgoing, 'expert', split_axis=0, concat_axis=0, tiled=True)  50.4 us
    all_to_all x1, blocking collectives, new_basis(): lax.all_to_all(outgoing, 'expert', split_axis=0, concat_axis=0, tiled=True)  48.9 us
    reduce_scatter x2, waiting for transfers between devices, new_basis(): lax.psum_scatter(by_cluster.astype(jnp.bfloat16), 'token', scatter_dimens...  43.4 us
  transfers between devices with their start and end apart: 9, of which 8 were waited for; matrix products, arithmetic and copies ran while one was open for 18% of the time, Pallas kernels for 0%

commit v1 on v0

v1 whole, which is shorter than its diff:
```python
import jax
import jax.numpy as jnp
from jax import lax
from jax.experimental import pallas as pl
from jax.experimental.pallas import tpu as pltpu
from jax.sharding import PartitionSpec as P

QUINTICS = (
    (6.009771924945882, -15.455931527233346, 10.973255328070678),
    (2.240850259026762, -1.6147116422452963, 0.4129695492489308),
    (1.8859120675161938, -1.2620718053405737, 0.3762092163333401),
)
DONE = 0.05**4
MOST = 60


def place_tokens(tok_rows, tok_ids, expert_count, capacity):
    flat_ids = tok_ids.reshape(-1)
    entry = jnp.arange(flat_ids.shape[0], dtype=jnp.int32)
    earlier = (flat_ids[:, None] == flat_ids[None, :]) & (entry[None, :] < entry[:, None])
    slot_index = jnp.sum(earlier.astype(jnp.int32), axis=1)
    target = flat_ids * capacity + slot_index
    select = (
        jnp.arange(expert_count * capacity, dtype=jnp.int32)[:, None] == target[None, :]
    ).astype(jnp.float32)
    select = (
        select.reshape(expert_count * capacity, tok_rows.shape[0], tok_ids.shape[1])
        .sum(axis=2)
        .astype(jnp.bfloat16)
    )
    filled = jnp.dot(select, tok_rows, preferred_element_type=jnp.float32).astype(jnp.bfloat16)
    return filled.reshape(expert_count, capacity, tok_rows.shape[1])


def dot16(a, b):
    return jnp.dot(
        a.astype(jnp.bfloat16), b.astype(jnp.bfloat16), preferred_element_type=jnp.float32
    )


def dot32(a, b, dims=(((1,), (0,)), ((), ()))):
    return lax.dot_general(
        a, b, dims, precision=lax.Precision.HIGHEST, preferred_element_type=jnp.float32
    )


def orthonormal_kernel(rows_ref, basis_ref, gram_ref, x_ref):
    rank = rows_ref.shape[1]
    gram = lax.dot_general(
        rows_ref[...], rows_ref[...], (((0,), (0,)), ((), ())), preferred_element_type=jnp.float32
    )
    eye = (
        lax.broadcasted_iota(jnp.int32, (rank, rank), 0)
        == lax.broadcasted_iota(jnp.int32, (rank, rank), 1)
    )
    diagonal = jnp.where(eye, gram, 0.0)
    down = lax.rsqrt(jnp.sum(diagonal, axis=1, keepdims=True))
    across = lax.rsqrt(jnp.sum(diagonal, axis=0, keepdims=True))
    gram = gram * down * across
    gram_ref[...] = gram
    rough = gram.astype(jnp.bfloat16)
    square = dot16(rough, rough)
    inv = lax.rsqrt(1.02 * jnp.sqrt(jnp.sum(square * square)))
    inv2 = inv * inv
    unit = eye.astype(jnp.float32)
    a, b, c = QUINTICS[0]
    x = inv * (a * unit + (b * inv2) * gram + (c * inv2 * inv2) * square)
    for a, b, c in QUINTICS[1:]:
        x16 = x.astype(jnp.bfloat16)
        s16 = dot16(x16, dot16(rough, x16)).astype(jnp.bfloat16)
        x = a * x + dot16(x16, b * s16.astype(jnp.float32) + c * dot16(s16, s16))
    x_ref[...] = x

    def unfinished(state):
        step, size = state
        return (size > DONE) & (step < MOST)

    def refine(state):
        step, _ = state
        x = x_ref[...]
        s = dot32(x, dot32(gram_ref[...], x), (((0,), (0,)), ((), ())))
        e = unit - s
        ee = dot16(e, e)
        x_ref[...] = x + dot16(x, 0.5 * e + 0.375 * ee)
        return step + 1, jnp.sum(ee * ee)

    lax.while_loop(unfinished, refine, (jnp.int32(0), jnp.float32(1.0)))
    scaled = x_ref[...] * down
    high = scaled.astype(jnp.bfloat16)
    low = (scaled - high.astype(jnp.float32)).astype(jnp.bfloat16)
    rows = rows_ref[...]
    basis_ref[...] = (
        jnp.dot(rows, high, preferred_element_type=jnp.float32)
        + jnp.dot(rows, low, preferred_element_type=jnp.float32)
    ).astype(jnp.bfloat16)


def orthonormal(cluster_rows):
    rank = cluster_rows.shape[1]
    return pl.pallas_call(
        orthonormal_kernel,
        out_shape=jax.ShapeDtypeStruct(cluster_rows.shape, jnp.bfloat16),
        in_specs=[pl.BlockSpec(memory_space=pltpu.VMEM)],
        out_specs=pl.BlockSpec(memory_space=pltpu.VMEM),
        scratch_shapes=[
            pltpu.VMEM((rank, rank), jnp.float32),
            pltpu.VMEM((rank, rank), jnp.float32),
        ],
        compiler_params=pltpu.CompilerParams(vmem_limit_bytes=48 << 20),
        cost_estimate=pl.CostEstimate(
            flops=40_000_000_000, bytes_accessed=4 << 20, transcendentals=0
        ),
        name="orthonormal",
    )(cluster_rows)


def new_basis(partial_term, same, token_count, expert_count):
    rows, rank = partial_term.shape
    block = rows // token_count // expert_count
    own = lax.psum_scatter(partial_term, "token", scatter_dimension=0, tiled=True)
    arrived = lax.all_to_all(
        own.reshape(expert_count, block * rank), "expert", split_axis=0, concat_axis=0, tiled=True
    )
    outgoing = jnp.dot(same, arrived, preferred_element_type=jnp.float32).astype(jnp.bfloat16)
    returned = lax.all_to_all(outgoing, "expert", split_axis=0, concat_axis=0, tiled=True)
    cluster_rows = lax.all_gather(
        returned.reshape(expert_count * block, rank), "token", axis=0, tiled=True
    )
    return orthonormal(cluster_rows)


def per_device(tokens, routes, assign, gate_weight, up_weight, sketch):
    expert_count = lax.axis_size("expert")
    token_count = lax.axis_size("token")
    gate_local = gate_weight[0]
    up_local = up_weight[0]
    same = (assign[None, :] == assign[:, None]).astype(jnp.bfloat16)
    partial_term = jnp.dot(up_local, sketch[0], preferred_element_type=jnp.float32).astype(
        jnp.bfloat16
    )
    basis = new_basis(partial_term, same, token_count, expert_count)
    projected = lax.dot_general(
        up_local, basis, (((0,), (0,)), ((), ())), preferred_element_type=jnp.float32
    ).astype(jnp.bfloat16)
    partial_term = jnp.dot(up_local, projected, preferred_element_type=jnp.float32).astype(
        jnp.bfloat16
    )
    basis = new_basis(partial_term, same, token_count, expert_count)
    shard_rows = tokens.shape[0]
    capacity = max(2, 2 * shard_rows * routes.shape[1] // expert_count)
    outgoing = place_tokens(tokens, routes, expert_count, capacity)
    arrived = lax.all_to_all(outgoing, "expert", split_axis=0, concat_axis=0, tiled=True)
    slots_in = lax.all_gather(arrived, "token", axis=0, tiled=True)
    slots_in = slots_in.reshape(-1, tokens.shape[1])
    gate_value = jnp.dot(slots_in, gate_local, preferred_element_type=jnp.float32)
    on_basis = jnp.dot(slots_in, basis, preferred_element_type=jnp.float32).astype(jnp.bfloat16)
    coefficient = lax.dot_general(
        basis, up_local, (((0,), (0,)), ((), ())), preferred_element_type=jnp.float32
    ).astype(jnp.bfloat16)
    merged = jnp.dot(on_basis, coefficient, preferred_element_type=jnp.float32)
    hidden = (jax.nn.silu(gate_value) * merged).astype(jnp.bfloat16)
    return hidden[None]


def solution(mesh):
    return jax.shard_map(
        per_device,
        mesh=mesh,
        in_specs=(
            P(("expert", "token"), None),
            P(("expert", "token"), None),
            P(),
            P("expert", None, "token"),
            P("expert", None, "token"),
            P("expert", "token", None),
        ),
        out_specs=P("expert", None, "token"),
        check_vma=False,
    )
```

time: 940 us -> 472 us (0.50)
  other arithmetic: 246 us -> 15.7 us
  waiting for transfers between devices: 243 us -> 91.3 us
  Pallas kernels: 0 us -> 42.1 us
  matrix products: 56.9 us -> 24 us
  blocking collectives: 280 us -> 248 us
  local copies, waits for them, and re-layouts: 58.5 us -> 28.2 us
  starting transfers between devices: 28 us -> 0.17 us
    another operation x35 -> x0, other arithmetic: 240 us -> none  [the longest x29 159 us: new_basis(): lower_factor = jnp.linalg.cholesky(column_gram)]
    all_to_all x2 -> x0, waiting for transfers between devices: 78.4 us -> none  [the longest x1 50.4 us: per_device(): lax.all_to_all(outgoing, 'expert', split_axis=0, concat_axis=0, tiled=True)]
    all_to_all x2 -> x3, blocking collectives: 231 us -> 168 us  [the longest x2 88 us: new_basis(): lax.all_to_all(own.reshape(expert_count, block * rank), 'expert', split_a...]
    psum x2 -> x0, waiting for transfers between devices: 51 us -> none  [new_basis(): lax.psum(local_gram.astype(jnp.bfloat16), 'token').astype(jnp.float32)]
    pallas_call x0 -> x2, Pallas kernels: none -> 42.1 us  [orthonormal(): pl.pallas_call(orthonormal_kernel, out_shape=jax.ShapeDtypeStruct(cluster...]
    all_to_all x1 -> x2, blocking collectives: 48.9 us -> 79.9 us  [new_basis(): lax.all_to_all(outgoing, 'expert', split_axis=0, concat_axis=0, tiled=True)]
    all_to_all x2 -> x0, starting transfers between devices: 27.4 us -> none  [the longest x1 18.3 us: new_basis(): lax.all_to_all(outgoing, 'expert', split_axis=0, concat_axis=0, tiled=True)]
    another operation x26 -> x0, matrix products: 24.7 us -> none  [the longest x14 13.8 us: new_basis(): jax.scipy.linalg.solve_triangular(lower_factor, cluster_rows.astype(jnp.f...]
  transfers between devices with their start and end apart: 9 -> 5, of which waited for: 8 -> 3; matrix products, arithmetic and copies ran while one was open for 18% -> 6% of each run, Pallas kernels for 0% -> 0%
where the time goes in v1:
time: 472 us; the launch traced here: 463 us
  blocking collectives  248 us (53%)
  waiting for transfers between devices  91.3 us (19%)
  Pallas kernels  42.1 us (9%)
  local copies, waits for them, and re-layouts  28.2 us (6%)
  matrix products  24 us (5%)
  other arithmetic  15.7 us (3%)
  between operations  13.8 us (3%)
    all_to_all x2, blocking collectives, new_basis(): lax.all_to_all(own.reshape(expert_count, block * rank), 'expert', split_a...  88 us
    all_to_all x1, blocking collectives, per_device(): lax.all_to_all(outgoing, 'expert', split_axis=0, concat_axis=0, tiled=True)  80 us
    all_to_all x2, blocking collectives, new_basis(): lax.all_to_all(outgoing, 'expert', split_axis=0, concat_axis=0, tiled=True)  79.9 us
    all_gather x2, waiting for transfers between devices, new_basis(): lax.all_gather(returned.reshape(expert_count * block, rank), 'token', axi...  48.4 us
    reduce_scatter x2, waiting for transfers between devices, new_basis(): lax.psum_scatter(partial_term, 'token', scatter_dimension=0, tiled=True)  42.8 us
    pallas_call x2, Pallas kernels, orthonormal(): pl.pallas_call(orthonormal_kernel, out_shape=jax.ShapeDtypeStruct(cluster...  42.1 us
    unnamed x29, local copies, waits for them, and re-layouts  11.5 us
  transfers between devices with their start and end apart: 5, of which 3 were waited for; matrix products, arithmetic and copies ran while one was open for 6% of the time, Pallas kernels for 0%

profile of v1, /device:TPU:1, one launch (start us, length us, event | category | flops | bytes accessed | tf_op | source)
XLA Modules:
  0.0 463.3 jit_solution(1308931197240194487)
XLA Ops:
  6.5 1.4 copy-done
  7.9 3.6 convolution_convert_fusion.1
  11.6 42.8 %reduce-scatter.3.cloned.1.call-done = bf16[512,512]{1,0:T(8,128)(2,1)} async-done(((bf16[2048,512]{1,0:T(8,128)(2,1)}), bf16[512,512]{1,0:T(8,128)(2,1)}) %reduce-scatter.3.cloned.1.call-update) | async-done | bytes 524304 | tf_op jit(solution)/shard_map/reduce_scatter | solution.py:120
  54.4 3.4 all_to_all.42
  58.4 3.7 reduce.2
  62.4 47.2 %all_to_all.49 = bf16[128,2,1024]{2,1,0:T(2,128)(2,1)S(1)} all-to-all(bf16[128,2,1024]{2,1,0:T(2,128)(2,1)S(1)} %reshape.54), channel_id=1, replica_groups=mesh['expert'=128,'token'=4] {'expert'}, dimensions={0} | all-to-all | bytes 1048576 | tf_op jit(solution)/shard_map/all_to_all | solution.py:121
  111.9 40.0 %all_to_all.50 = bf16[128,2,1024]{2,1,0:T(2,128)(2,1)S(1)} all-to-all(bf16[128,2,1024]{2,1,0:T(2,128)(2,1)S(1)} %reshape.56), channel_id=1, replica_groups=mesh['expert'=128,'token'=4] {'expert'}, dimensions={0} | all-to-all | bytes 1048576 | tf_op jit(solution)/shard_map/all_to_all | solution.py:125
  152.4 3.1 reduce
  157.2 30.3 %all-gather.6.cloned.1.call-done.rows_ref = bf16[2048,512]{1,0:T(8,128)(2,1)} async-done(((bf16[512,512]{1,0:T(8,128)(2,1)}), bf16[2048,512]{1,0:T(8,128)(2,1)}) %all-gather.6.cloned.1.call-update) | async-done | bytes 2097168 | tf_op jit(solution)/shard_map/all_gather | solution.py:126
  187.5 1.6 copy-done.2
  189.1 25.3 %orthonormal.2 = bf16[2048,512]{1,0:T(8,128)(2,1)S(1)} custom-call(bf16[2048,512]{1,0:T(8,128)(2,1)S(1)} %copy-done.2), custom_call_target="tpu_custom_call" | custom-call | flops 40000000000 | bytes 4194304 | tf_op jit(solution)/shard_map/orthonormal/pallas_call | solution.py:100
  215.8 5.3 %fusion = bf16[2048,512]{0,1:T(8,128)(2,1)} fusion(bf16[1,2048,384]{2,1,0:T(8,128)(2,1)S(1)} %copy-done, bf16[2048,512]{1,0:T(8,128)(2,1)} %copy-done.4), kind=kOutput, calls=%fused_computation.2 | convolution fusion | flops 1611857920 | bytes 5767168 | tf_op jit(solution)/shard_map/dot_general | solution.py:145
  222.3 1.5 reshape.48
  223.9 80.0 %all_to_all.51 = bf16[128,2,2048]{2,1,0:T(2,128)(2,1)} all-to-all(bf16[128,2,2048]{2,1,0:T(2,128)(2,1)} %reshape.48), channel_id=1, replica_groups=mesh['expert'=128,'token'=4] {'expert'}, dimensions={0} | all-to-all | bytes 2097152 | tf_op jit(solution)/shard_map/all_to_all | solution.py:152
  305.5 3.7 reduce.4
  309.6 40.8 %all_to_all.52 = bf16[128,2,1024]{2,1,0:T(2,128)(2,1)S(1)} all-to-all(bf16[128,2,1024]{2,1,0:T(2,128)(2,1)S(1)} %reshape.58), channel_id=1, replica_groups=mesh['expert'=128,'token'=4] {'expert'}, dimensions={0} | all-to-all | bytes 1048576 | tf_op jit(solution)/shard_map/all_to_all | solution.py:121
  352.7 39.9 %all_to_all.53 = bf16[128,2,1024]{2,1,0:T(2,128)(2,1)S(1)} all-to-all(bf16[128,2,1024]{2,1,0:T(2,128)(2,1)S(1)} %reshape.60), channel_id=1, replica_groups=mesh['expert'=128,'token'=4] {'expert'}, dimensions={0} | all-to-all | bytes 1048576 | tf_op jit(solution)/shard_map/all_to_all | solution.py:125
  393.1 3.1 reduce.1
  397.3 7.3 %reshape.49 = bf16[1024,2048]{1,0:T(8,128)(2,1)} reshape(bf16[512,2,2048]{2,1,0:T(2,128)(2,1)} %all-gather.4.cloned.1.call-done) | data formatting | bytes 8388608 | tf_op jit(solution)/shard_map/reshape | solution.py:154
  404.6 5.7 %fusion.9 = f32[1024,384]{1,0:T(8,128)} fusion(bf16[1024,2048]{1,0:T(8,128)(2,1)} %reshape.49, bf16[1,2048,384]{2,1,0:T(8,128)(2,1)S(1)} %copy-done.8), kind=kOutput, calls=%fused_computation.14 | convolution fusion | flops 1610612736 | bytes 7340032 | tf_op jit(solution)/shard_map/dot_general | solution.py:155
  410.4 18.1 %all-gather.8.cloned.1.call-done.rows_ref = bf16[2048,512]{1,0:T(8,128)(2,1)} async-done(((bf16[512,512]{1,0:T(8,128)(2,1)}), bf16[2048,512]{1,0:T(8,128)(2,1)}) %all-gather.8.cloned.1.call-update) | async-done | bytes 2097168 | tf_op jit(solution)/shard_map/all_gather | solution.py:126
  428.5 1.6 copy-done.3
  430.1 16.7 %orthonormal.3 = bf16[2048,512]{1,0:T(8,128)(2,1)S(1)} custom-call(bf16[2048,512]{1,0:T(8,128)(2,1)S(1)} %copy-done.3), custom_call_target="tpu_custom_call" | custom-call | flops 40000000000 | bytes 4194304 | tf_op jit(solution)/shard_map/orthonormal/pallas_call | solution.py:100
  449.6 6.7 %fusion.11 = bf16[1,1024,384]{2,1,0:T(8,128)(2,1)} fusion(bf16[512,384]{1,0:T(8,128)(2,1)S(1)} %fusion.15, f32[1024,384]{1,0:T(8,128)S(1)} %copy-done.9, bf16[1024,2048]{1,0:T(8,128)(2,1)} %reshape.49, bf16[2048,512]{1,0:T(8,128)(2,1)} %copy-done.1), kind=kOutput, calls=%fused_computation.18 | convolution fusion | flops 2553020416 | bytes 9043968 | tf_op jit(solution)/shard_map/dot_general | solution.py:160
  (54 shorter events, 16.7 us)
Async XLA Ops:
  6.5 1.4 copy-start
  6.5 47.9 %reduce-scatter.3.cloned.1.call-start = ((), (), s32[]{:S(2)}) async-start(), calls=%async_computation.8 | async-start | bytes 2621440 | tf_op jit(solution)/shard_map/reduce_scatter | solution.py:120
  11.6 175.9 %all-gather.6.cloned.1.call-start = ((), (), s32[]{:S(2)}) async-start(), calls=%async_computation.9 | async-start | bytes 2621440 | tf_op jit(solution)/shard_map/all_gather | solution.py:126
  62.1 48.0 %copy-start.6 = (s32[128]{0:T(128)S(1)}, s32[128]{0:T(128)}, u32[]{:S(2)}) copy-start(s32[128]{0:T(128)} %param.8) | copy-start | bytes 1540
  151.9 4.7 %copy-start.7 = (s32[16,8]{0,1:T(8,128)S(1)}, s32[16,8]{0,1:T(8,128)}, u32[]{:S(2)}) copy-start(s32[16,8]{0,1:T(8,128)} %param.7) | copy-start | bytes 1540
  156.6 147.4 %reduce-scatter.5.cloned.1.call-start = ((), (), s32[]{:S(2)}) async-start(), calls=%async_computation.10 | async-start | bytes 2621440 | tf_op jit(solution)/shard_map/reduce_scatter | solution.py:120
  187.5 1.6 copy-start.2
  214.4 1.4 copy-start.4
  221.0 0.8 copy-start.5
  221.1 176.2 %all-gather.4.cloned.1.call-start = ((), (), s32[]{:S(2)}) async-start(), calls=%async_computation.7 | async-start | bytes 5242880 | tf_op jit(solution)/shard_map/all_gather | solution.py:153
  303.9 124.6 %all-gather.8.cloned.1.call-start = ((), (), s32[]{:S(2)}) async-start(), calls=%async_computation.11 | async-start | bytes 2621440 | tf_op jit(solution)/shard_map/all_gather | solution.py:126
  397.3 7.4 %copy-start.8 = (bf16[1,2048,384]{2,1,0:T(8,128)(2,1)S(1)}, bf16[1,2048,384]{2,1,0:T(8,128)(2,1)}, u32[]{:S(2)}) copy-start(bf16[1,2048,384]{2,1,0:T(8,128)(2,1)} %param.9) | copy-start | bytes 4718596
  428.5 1.6 copy-start.3
  446.8 1.4 copy-start.1
  448.2 1.4 copy-start.9
Sparse Core Ops, SparseCore 0:
  11.7 42.6 reduce-scatter.2
  156.7 30.7 all-gather.5
  221.2 40.8 reduce-scatter.4
  304.0 49.5 all-gather.3
  397.4 31.0 all-gather.7

commit v2 on v1

--- a/solution.py
+++ b/solution.py
@@ -4,6 +4,8 @@
 from jax.experimental import pallas as pl
 from jax.experimental.pallas import tpu as pltpu
 from jax.sharding import PartitionSpec as P
+
+MESH = pl.DeviceIdType.MESH
 
 QUINTICS = (
     (6.009771924945882, -15.455931527233346, 10.973255328070678),
@@ -114,38 +116,250 @@
     )(cluster_rows)
 
 
-def new_basis(partial_term, same, token_count, expert_count):
+CHUNKS = 4
+TILE = (16, 128)
+
+
+def exchange_kernel(
+    part, same, out, heard, pairs, met, own, tiles, tiles32, mixed32, mixed,
+    first_sent, first_got, second_sent, second_got, out_sent, out_got, back_sent, back_got,
+    share_sent, share_got,
+):
+    experts, n_token = lax.axis_size("expert"), lax.axis_size("token")
+    me, t = lax.axis_index("expert"), lax.axis_index("token")
+    near, far = t + 1 - 2 * (t % 2), n_token - 1 - t
+    block = part.shape[0] // n_token
+    half = part.shape[1] // 2
+    step = block // CHUNKS
+    tile_rows, tile_cols = TILE
+    halves = (pl.ds(0, half), pl.ds(half, half))
+
+    def place(expert):
+        core, chip = expert % 2, expert // 2
+        y, z = chip % 4, chip // 4
+        return core + 2 * (z % 2), z // 2, y
+
+    def expert_at(chunk, deep, y):
+        return ((2 * deep + chunk // 2) * 4 + y) * 2 + chunk % 2
+
+    def tile_at(base, chunk, deep, y):
+        row = pl.multiple_of(base + chunk * step + deep * tile_rows, tile_rows)
+        return pl.ds(row, tile_rows), pl.ds(pl.multiple_of(y * tile_cols, tile_cols), tile_cols)
+
+    def rows_of(owner, chunk):
+        return pl.ds(pl.multiple_of(owner * block + chunk * step, step), step)
+
+    def send(src, dst, sent, got, device):
+        return pltpu.make_async_remote_copy(
+            src_ref=src, dst_ref=dst, send_sem=sent, recv_sem=got,
+            device_id=device, device_id_type=MESH,
+        )
+
+    barrier = pltpu.get_barrier_semaphore()
+
+    def greet(i, carry):
+        pl.semaphore_signal(
+            barrier, inc=1, device_id=((me + i) % experts, t), device_id_type=MESH
+        )
+        return carry
+
+    for other in (near, far):
+        pl.semaphore_signal(barrier, inc=1, device_id=(me, other), device_id_type=MESH)
+    lax.fori_loop(1, experts, greet, 0)
+    pl.semaphore_wait(barrier, experts + 1)
+
+    def first(chunk, side, slot):
+        to = (near, far)[side]
+        owner = (to, (n_token - 1 - to, to + 1 - 2 * (to % 2))[side])[slot]
+        return send(
+            part.at[rows_of(owner, chunk), halves[side]], heard.at[side, chunk, slot],
+            first_sent.at[side, chunk, slot], first_got.at[side, chunk, slot], (me, to),
+        )
+
+    def second(chunk, side):
+        return send(
+            pairs.at[side, chunk], met.at[side, chunk],
+            second_sent.at[side, chunk], second_got.at[side, chunk], (me, (far, near)[side]),
+        )
+
+    def start_first(chunk, carry):
+        for side in range(2):
+            for slot in (1, 0):
+                first(chunk, side, slot).start()
+        return carry
+
+    def start_second(chunk):
+        for side in range(2):
+            first(chunk, side, 1).wait_recv()
+            pairs[side, chunk] = (
+                part[rows_of((far, near)[side], chunk), halves[side]].astype(jnp.float32)
+                + heard[side, chunk, 1].astype(jnp.float32)
+            ).astype(jnp.bfloat16)
+            second(chunk, side).start()
+
+    def scatter(chunk):
+        for side in range(2):
+            first(chunk, side, 0).wait_recv()
+            second(chunk, side).wait_recv()
+            own[pl.ds(pl.multiple_of(chunk * step, step), step), halves[side]] = (
+                part[rows_of(t, chunk), halves[side]].astype(jnp.float32)
+                + heard[side, chunk, 0].astype(jnp.float32)
+                + met[side, chunk].astype(jnp.float32)
+            ).astype(jnp.bfloat16)
+        count = experts // CHUNKS
+
+        def one(i, carry):
+            spot = (i + me) % count
+            deep, y = spot // 4, spot % 4
+            to = expert_at(chunk, deep, y)
+            rows, cols = tile_at(0, chunk, deep, y)
+
+            @pl.when(to != me)
+            def _():
+                send(own.at[rows, cols], tiles.at[me], out_sent, out_got, (to, t)).start()
+
+            @pl.when(to == me)
+            def _():
+                pltpu.make_async_copy(own.at[rows, cols], tiles.at[me], out_got).start()
+
+            return carry
+
+        lax.fori_loop(0, count, one, 0)
+
+    lax.fori_loop(0, CHUNKS, start_first, 0)
+    start_second(0)
+
+    def along(chunk, carry):
+        start_second(chunk)
+        scatter(chunk - 1)
+        return carry
+
+    lax.fori_loop(1, CHUNKS, along, 0)
+    scatter(CHUNKS - 1)
+
+    pltpu.make_async_copy(tiles, tiles, out_got).wait()
+    tiles32[...] = tiles[...].reshape(tiles32.shape).astype(jnp.float32)
+    for r in range(tile_rows):
+        every = pl.ds(r, experts, stride=tile_rows)
+        mixed32[every, :] = jnp.dot(
+            same[...], tiles32[every, :].astype(jnp.bfloat16), preferred_element_type=jnp.float32
+        )
+    mixed[...] = mixed32[...].astype(jnp.bfloat16).reshape(mixed.shape)
+
+    my_chunk, my_deep, my_y = place(me)
+    my_rows, my_cols = tile_at(t * block, my_chunk, my_deep, my_y)
+
+    def give(i, carry):
+        to = (me + i) % experts
+        send(
+            mixed.at[to], out.at[my_rows, my_cols], back_sent, back_got.at[my_chunk], (to, t)
+        ).start()
+        return carry
+
+    pltpu.make_async_copy(mixed.at[me], out.at[my_rows, my_cols], back_got.at[my_chunk]).start()
+    lax.fori_loop(1, experts, give, 0)
+
+    def share(chunk, kind):
+        owner = (t, t, near, far)[kind]
+        cols = (pl.ds(0, 2 * half), pl.ds(0, 2 * half), halves[0], halves[1])[kind]
+        spot = out.at[rows_of(owner, chunk), cols]
+        to = (near, far, far, near)[kind]
+        return send(spot, spot, share_sent.at[kind, chunk], share_got.at[kind, chunk], (me, to))
+
+    def start_share(chunk):
+        mine = out.at[rows_of(t, chunk), :]
+        pltpu.make_async_copy(mine, mine, back_got.at[chunk]).wait()
+        share(chunk, 0).start()
+        share(chunk, 1).start()
+
+    def pass_on(chunk):
+        share(chunk, 0).wait_recv()
+        share(chunk, 2).start()
+        share(chunk, 1).wait_recv()
+        share(chunk, 3).start()
+
+    start_share(0)
+
+    def gather(chunk, carry):
+        start_share(chunk)
+        pass_on(chunk - 1)
+        return carry
+
+    lax.fori_loop(1, CHUNKS, gather, 0)
+    pass_on(CHUNKS - 1)
+
+    def finish(chunk, carry):
+        for kind in (2, 3):
+            share(chunk, kind).wait_recv()
+        for kind in range(4):
+            share(chunk, kind).wait_send()
+        for side in range(2):
+            second(chunk, side).wait_send()
+            for slot in range(2):
+                first(chunk, side, slot).wait_send()
+        return carry
+
+    lax.fori_loop(0, CHUNKS, finish, 0)
+    most = tiles.at[pl.ds(0, experts - 1)]
+    pltpu.make_async_copy(most, most, out_sent).wait()
+    pltpu.make_async_copy(most, most, back_sent).wait()
+
+
+def exchange(partial_term, same):
     rows, rank = partial_term.shape
-    block = rows // token_count // expert_count
-    own = lax.psum_scatter(partial_term, "token", scatter_dimension=0, tiled=True)
-    arrived = lax.all_to_all(
-        own.reshape(expert_count, block * rank), "expert", split_axis=0, concat_axis=0, tiled=True
-    )
-    outgoing = jnp.dot(same, arrived, preferred_element_type=jnp.float32).astype(jnp.bfloat16)
-    returned = lax.all_to_all(outgoing, "expert", split_axis=0, concat_axis=0, tiled=True)
-    cluster_rows = lax.all_gather(
-        returned.reshape(expert_count * block, rank), "token", axis=0, tiled=True
-    )
-    return orthonormal(cluster_rows)
+    experts, n_token = lax.axis_size("expert"), lax.axis_size("token")
+    block, half = rows // n_token, rank // 2
+    step = block // CHUNKS
+    tile_rows, tile_cols = TILE
+    vmem = pl.BlockSpec(memory_space=pltpu.VMEM)
+    dma = pltpu.SemaphoreType.DMA
+    return pl.pallas_call(
+        exchange_kernel,
+        out_shape=jax.ShapeDtypeStruct((rows, rank), jnp.bfloat16),
+        in_specs=[vmem, vmem],
+        out_specs=vmem,
+        scratch_shapes=[
+            pltpu.VMEM((2, CHUNKS, 2, step, half), jnp.bfloat16),
+            pltpu.VMEM((2, CHUNKS, step, half), jnp.bfloat16),
+            pltpu.VMEM((2, CHUNKS, step, half), jnp.bfloat16),
+            pltpu.VMEM((block, rank), jnp.bfloat16),
+            pltpu.VMEM((experts, tile_rows, tile_cols), jnp.bfloat16),
+            pltpu.VMEM((experts * tile_rows, tile_cols), jnp.float32),
+            pltpu.VMEM((experts * tile_rows, tile_cols), jnp.float32),
+            pltpu.VMEM((experts, tile_rows, tile_cols), jnp.bfloat16),
+            dma((2, CHUNKS, 2)), dma((2, CHUNKS, 2)), dma((2, CHUNKS)), dma((2, CHUNKS)),
+            dma, dma, dma, dma((CHUNKS,)), dma((4, CHUNKS)), dma((4, CHUNKS)),
+        ],
+        compiler_params=pltpu.CompilerParams(
+            collective_id=0, has_side_effects=True, vmem_limit_bytes=40 << 20
+        ),
+        cost_estimate=pl.CostEstimate(
+            flops=60_000_000_000, bytes_accessed=8 << 20, transcendentals=0
+        ),
+        name="exchange",
+    )(partial_term, same)
+
+
+def new_basis(partial_term, same):
+    return orthonormal(exchange(partial_term, same))
 
 
 def per_device(tokens, routes, assign, gate_weight, up_weight, sketch):
     expert_count = lax.axis_size("expert")
-    token_count = lax.axis_size("token")
     gate_local = gate_weight[0]
     up_local = up_weight[0]
     same = (assign[None, :] == assign[:, None]).astype(jnp.bfloat16)
     partial_term = jnp.dot(up_local, sketch[0], preferred_element_type=jnp.float32).astype(
         jnp.bfloat16
     )
-    basis = new_basis(partial_term, same, token_count, expert_count)
+    basis = new_basis(partial_term, same)
     projected = lax.dot_general(
         up_local, basis, (((0,), (0,)), ((), ())), preferred_element_type=jnp.float32
     ).astype(jnp.bfloat16)
     partial_term = jnp.dot(up_local, projected, preferred_element_type=jnp.float32).astype(
         jnp.bfloat16
     )
-    basis = new_basis(partial_term, same, token_count, expert_count)
+    basis = new_basis(partial_term, same)
     shard_rows = tokens.shape[0]
     capacity = max(2, 2 * shard_rows * routes.shape[1] // expert_count)
     outgoing = place_tokens(tokens, routes, expert_count, capacity)

time: 472 us -> 333 us (0.71)
  blocking collectives: 248 us -> 0 us
  Pallas kernels: 42.1 us -> 255 us
  waiting for transfers between devices: 91.3 us -> 0.04 us
  starting transfers between devices: 0.17 us -> 20.8 us
  other arithmetic: 15.7 us -> 0.4 us
  local copies, waits for them, and re-layouts: 28.2 us -> 15.2 us
    all_to_all x5 -> x0, blocking collectives: 248 us -> none  [the longest x2 88 us: new_basis(): lax.all_to_all(own.reshape(expert_count, block * rank), 'expert', split_a...]
    pallas_call x0 -> x2, Pallas kernels: none -> 213 us  [exchange(): pl.pallas_call(exchange_kernel, out_shape=jax.ShapeDtypeStruct((rows, ran...]
    all_gather x2 -> x0, waiting for transfers between devices: 48.4 us -> none  [new_basis(): lax.all_gather(returned.reshape(expert_count * block, rank), 'token', axi...]
    reduce_scatter x2 -> x0, waiting for transfers between devices: 42.8 us -> none  [new_basis(): lax.psum_scatter(partial_term, 'token', scatter_dimension=0, tiled=True)]
    all_to_all x0 -> x1, starting transfers between devices: none -> 20.6 us  [per_device(): lax.all_to_all(outgoing, 'expert', split_axis=0, concat_axis=0, tiled=True)]
    all_to_all x6 -> x0, other arithmetic: 15.4 us -> none  [the longest x4 8.06 us: new_basis(): lax.all_to_all(outgoing, 'expert', split_axis=0, concat_axis=0, tiled=True)]
    unnamed x29 -> x17, local copies, waits for them, and re-layouts: 11.5 us -> 6.17 us
  transfers between devices with their start and end apart: 5 -> 2, of which waited for: 3 -> 0; matrix products, arithmetic and copies ran while one was open for 6% -> 2% of each run, Pallas kernels for 0% -> 78%
where the time goes in v2:
time: 333 us; the launch traced here: 327 us
  Pallas kernels  255 us (77%)
  matrix products  22 us (7%)
  starting transfers between devices  20.8 us (6%)
  local copies, waits for them, and re-layouts  15.2 us (5%)
  between operations  13.6 us (4%)
    pallas_call x2, Pallas kernels, exchange(): pl.pallas_call(exchange_kernel, out_shape=jax.ShapeDtypeStruct((rows, ran...  213 us
    pallas_call x2, Pallas kernels, orthonormal(): pl.pallas_call(orthonormal_kernel, out_shape=jax.ShapeDtypeStruct(cluster...  42.3 us
    all_to_all x1, starting transfers between devices, per_device(): lax.all_to_all(outgoing, 'expert', split_axis=0, concat_axis=0, tiled=True)  20.6 us
    reshape x1, local copies, waits for them, and re-layouts, per_device(): slots_in = slots_in.reshape(-1, tokens.shape[1])  7.34 us
    dot_general x1, matrix products, per_device(): merged = jnp.dot(on_basis, coefficient, preferred_element_type=jnp.float32)  7.08 us
  transfers between devices with their start and end apart: 2, of which 0 were waited for; matrix products, arithmetic and copies ran while one was open for 2% of the time, Pallas kernels for 78%

profile of v2, /device:TPU:1, one launch (start us, length us, event | category | flops | bytes accessed | tf_op | source)
XLA Modules:
  0.0 327.2 jit_solution(14284808016974816627)
XLA Ops:
  6.5 0.9 copy.16
  7.4 0.1 eq.43
  7.5 0.2 convert_reduce_fusion.1
  7.7 0.1 reduce_sum.21
  7.8 0.1 convert_reduce_fusion
  7.9 1.3 convolution_convert_fusion.2
  9.2 1.5 reshape.28
  10.8 20.6 %all-to-all-start = ((bf16[128,2,2048]{2,1,0:T(2,128)(2,1)}), bf16[128,2,2048]{2,1,0:T(2,128)(2,1)S(1)}, u32[]{:S(2)}, u32[]{:S(2)}) async-start(bf16[128,2,2048]{2,1,0:T(2,128)(2,1)} %reshape.28), calls=%async_computation | async-start | bytes 2097152 | tf_op jit(solution)/shard_map/all_to_all | solution.py:366
  31.3 0.2 all-gather.2.cloned.1.call-start
  31.6 0.1 compare_convert_fusion.same
  31.7 1.2 convolution_convert_fusion.1.part
  32.9 115.4 %exchange.2.rows_ref = bf16[2048,512]{1,0:T(8,128)(2,1)S(1)} custom-call(bf16[2048,512]{1,0:T(8,128)(2,1)S(1)} %convolution_convert_fusion.1.part, bf16[128,128]{1,0:T(8,128)(2,1)S(1)} %compare_convert_fusion.same), custom_call_target="tpu_custom_call" | custom-call | flops 60000002048 | bytes 8388608 | tf_op jit(solution)/shard_map/exchange/pallas_call | solution.py:316
  148.3 30.0 %orthonormal.2 = bf16[2048,512]{1,0:T(8,128)(2,1)S(1)} custom-call(bf16[2048,512]{1,0:T(8,128)(2,1)S(1)} %exchange.2.rows_ref), custom_call_target="tpu_custom_call" | custom-call | flops 40000000000 | bytes 4194304 | tf_op jit(solution)/shard_map/orthonormal/pallas_call | solution.py:102
  178.3 1.3 copy-done.3
  179.6 5.4 %fusion.part = bf16[2048,512]{1,0:T(8,128)(2,1)} fusion(bf16[1,2048,384]{2,1,0:T(8,128)(2,1)S(1)} %copy-done, bf16[2048,512]{1,0:T(8,128)(2,1)} %copy-done.3), kind=kOutput, calls=%fused_computation.2 | convolution fusion | flops 1611857920 | bytes 5767168 | tf_op jit(solution)/shard_map/dot_general | solution.py:359
  185.1 1.0 copy-done.4
  186.1 1.6 copy-done.2
  187.7 97.6 %exchange.3.rows_ref = bf16[2048,512]{1,0:T(8,128)(2,1)S(1)} custom-call(bf16[2048,512]{1,0:T(8,128)(2,1)S(1)} %copy-done.2, bf16[128,128]{1,0:T(8,128)(2,1)S(1)} %compare_convert_fusion.same), custom_call_target="tpu_custom_call" | custom-call | flops 60000002048 | bytes 8388608 | tf_op jit(solution)/shard_map/exchange/pallas_call | solution.py:316
  285.3 12.3 %orthonormal.3 = bf16[2048,512]{1,0:T(8,128)(2,1)S(1)} custom-call(bf16[2048,512]{1,0:T(8,128)(2,1)S(1)} %exchange.3.rows_ref), custom_call_target="tpu_custom_call" | custom-call | flops 40000000000 | bytes 4194304 | tf_op jit(solution)/shard_map/orthonormal/pallas_call | solution.py:102
  297.6 1.3 copy-done.1
  299.0 1.3 fusion.13
  300.3 7.3 %reshape.29 = bf16[1024,2048]{1,0:T(8,128)(2,1)} reshape(bf16[512,2,2048]{2,1,0:T(2,128)(2,1)} %all-gather.2.cloned.1.call-done) | data formatting | bytes 8388608 | tf_op jit(solution)/shard_map/reshape | solution.py:368
  307.6 5.7 %fusion.7 = f32[1024,384]{1,0:T(8,128)} fusion(bf16[1024,2048]{1,0:T(8,128)(2,1)} %reshape.29, bf16[1,2048,384]{2,1,0:T(8,128)(2,1)S(1)} %copy-done.6), kind=kOutput, calls=%fused_computation.10 | convolution fusion | flops 1610612736 | bytes 7340032 | tf_op jit(solution)/shard_map/dot_general | solution.py:369
  313.3 7.1 %fusion.9 = bf16[1,1024,384]{2,1,0:T(8,128)(2,1)} fusion(bf16[512,384]{1,0:T(8,128)(2,1)S(1)} %fusion.13, f32[1024,384]{1,0:T(8,128)} %fusion.7, bf16[1024,2048]{1,0:T(8,128)(2,1)} %reshape.29, bf16[2048,512]{1,0:T(8,128)(2,1)} %copy-done.1), kind=kOutput, calls=%fused_computation.14 | convolution fusion | flops 2553020416 | bytes 9043968 | tf_op jit(solution)/shard_map/dot_general | solution.py:374
  (16 shorter events, 0.1 us)
Async XLA Ops:
  6.5 25.1 %copy-start = (bf16[1,2048,384]{2,1,0:T(8,128)(2,1)S(1)}, bf16[1,2048,384]{2,1,0:T(8,128)(2,1)}, u32[]{:S(2)}) copy-start(bf16[1,2048,384]{2,1,0:T(8,128)(2,1)} %param.10) | copy-start | bytes 4718596
  9.2 22.3 %copy-start.5 = (s32[128]{0:T(128)S(1)}, s32[128]{0:T(128)}, u32[]{:S(2)}) copy-start(s32[128]{0:T(128)} %param.8) | copy-start | bytes 1540
  9.2 22.4 %copy-start.7 = (bf16[1,384,512]{2,1,0:T(8,128)(2,1)S(1)}, bf16[1,384,512]{2,1,0:T(8,128)(2,1)}, u32[]{:S(2)}) copy-start(bf16[1,384,512]{2,1,0:T(8,128)(2,1)} %param.11) | copy-start | bytes 1179652
  10.8 174.3 %all-to-all-start = ((bf16[128,2,2048]{2,1,0:T(2,128)(2,1)}), bf16[128,2,2048]{2,1,0:T(2,128)(2,1)S(1)}, u32[]{:S(2)}, u32[]{:S(2)}) async-start(bf16[128,2,2048]{2,1,0:T(2,128)(2,1)} %reshape.28), calls=%async_computation | async-start | bytes 2097152 | tf_op jit(solution)/shard_map/all_to_all | solution.py:366
  31.3 269.0 %all-gather.2.cloned.1.call-start = ((), (), s32[]{:S(2)}) async-start(), calls=%async_computation.1 | async-start | bytes 5242880 | tf_op jit(solution)/shard_map/all_gather | solution.py:367
  178.3 1.3 copy-start.3
  185.1 1.0 copy-start.4
  186.1 1.6 copy-start.2
  297.6 1.4 copy-start.1
  300.3 7.4 %copy-start.6 = (bf16[1,2048,384]{2,1,0:T(8,128)(2,1)S(1)}, bf16[1,2048,384]{2,1,0:T(8,128)(2,1)}, u32[]{:S(2)}) copy-start(bf16[1,2048,384]{2,1,0:T(8,128)(2,1)} %param.9) | copy-start | bytes 4718596
Sparse Core Ops, SparseCore 0:
  186.2 65.5 all-gather.1

commit v3 on v2

--- a/solution.py
+++ b/solution.py
@@ -12,26 +12,31 @@
     (2.240850259026762, -1.6147116422452963, 0.4129695492489308),
     (1.8859120675161938, -1.2620718053405737, 0.3762092163333401),
 )
-DONE = 0.05**4
+DONE = 0.01**2
 MOST = 60
-
-
-def place_tokens(tok_rows, tok_ids, expert_count, capacity):
-    flat_ids = tok_ids.reshape(-1)
-    entry = jnp.arange(flat_ids.shape[0], dtype=jnp.int32)
-    earlier = (flat_ids[:, None] == flat_ids[None, :]) & (entry[None, :] < entry[:, None])
-    slot_index = jnp.sum(earlier.astype(jnp.int32), axis=1)
-    target = flat_ids * capacity + slot_index
-    select = (
-        jnp.arange(expert_count * capacity, dtype=jnp.int32)[:, None] == target[None, :]
-    ).astype(jnp.float32)
-    select = (
-        select.reshape(expert_count * capacity, tok_rows.shape[0], tok_ids.shape[1])
-        .sum(axis=2)
-        .astype(jnp.bfloat16)
-    )
-    filled = jnp.dot(select, tok_rows, preferred_element_type=jnp.float32).astype(jnp.bfloat16)
-    return filled.reshape(expert_count, capacity, tok_rows.shape[1])
+OVER_ROWS = (((0,), (0,)), ((), ()))
+SLOT_ROWS = 256
+
+
+def own_slots(tokens, routes):
+    expert_count = lax.axis_size("expert")
+    rows, width = tokens.shape
+    top = routes.shape[1]
+    capacity = max(2, 2 * rows * top // expert_count)
+    marked = jnp.pad(routes.astype(jnp.bfloat16), ((0, 0), (0, 128 - top)), constant_values=-1)
+    every = lax.all_gather(
+        jnp.concatenate([tokens, marked], axis=1), "expert", axis=0, tiled=True
+    )
+    me = lax.axis_index("expert").astype(jnp.bfloat16)
+    named = jnp.any(every[:, width:] == me, axis=1).reshape(expert_count, rows)
+    before = jnp.arange(rows)[:, None] < jnp.arange(rows)[None, :]
+    slot = jnp.sum((named[:, :, None] & before[None]).astype(jnp.int32), axis=1)
+    target = jnp.arange(expert_count, dtype=jnp.int32)[:, None] * capacity + slot
+    target = jnp.where(named & (slot < capacity), target, -1).reshape(1, -1)
+    place = jnp.arange(expert_count * capacity, dtype=jnp.int32)[:, None]
+    select = (place == target).astype(jnp.bfloat16)
+    picked = jnp.dot(select, every, preferred_element_type=jnp.float32)
+    return picked[:, :width].astype(jnp.bfloat16)
 
 
 def dot16(a, b):
@@ -46,7 +51,7 @@
     )
 
 
-def orthonormal_kernel(rows_ref, basis_ref, gram_ref, x_ref):
+def orthonormal(rows_ref, basis_ref, gram_ref, x_ref):
     rank = rows_ref.shape[1]
     gram = lax.dot_general(
         rows_ref[...], rows_ref[...], (((0,), (0,)), ((), ())), preferred_element_type=jnp.float32
@@ -97,31 +102,65 @@
     ).astype(jnp.bfloat16)
 
 
-def orthonormal(cluster_rows):
-    rank = cluster_rows.shape[1]
+def gram_kernel(rows_ref, up_ref, projected_ref, basis_ref, gram_ref, x_ref):
+    orthonormal(rows_ref, basis_ref, gram_ref, x_ref)
+    projected_ref[...] = lax.dot_general(
+        up_ref[...], basis_ref[...], OVER_ROWS, preferred_element_type=jnp.float32
+    ).astype(jnp.bfloat16)
+
+
+def hidden_kernel(
+    rows_ref, up_ref, gate_ref, slots_ref, hidden_ref, basis_ref, gram_ref, x_ref, coefficient_ref
+):
+    orthonormal(rows_ref, basis_ref, gram_ref, x_ref)
+    coefficient_ref[...] = lax.dot_general(
+        basis_ref[...], up_ref[...], OVER_ROWS, preferred_element_type=jnp.float32
+    ).astype(jnp.bfloat16)
+
+    def some(i, carry):
+        these = pl.ds(pl.multiple_of(i * SLOT_ROWS, SLOT_ROWS), SLOT_ROWS)
+        slots = slots_ref[these, :]
+        gate = jnp.dot(slots, gate_ref[...], preferred_element_type=jnp.float32)
+        on_basis = jnp.dot(slots, basis_ref[...], preferred_element_type=jnp.float32)
+        merged = jnp.dot(
+            on_basis.astype(jnp.bfloat16),
+            coefficient_ref[...],
+            preferred_element_type=jnp.float32,
+        )
+        hidden_ref[these, :] = (gate / (1.0 + jnp.exp(-gate)) * merged).astype(jnp.bfloat16)
+        return carry
+
+    lax.fori_loop(0, slots_ref.shape[0] // SLOT_ROWS, some, 0)
+
+
+def with_basis(kernel, name, out, rank, more, *operands):
+    vmem = pl.BlockSpec(memory_space=pltpu.VMEM)
     return pl.pallas_call(
-        orthonormal_kernel,
-        out_shape=jax.ShapeDtypeStruct(cluster_rows.shape, jnp.bfloat16),
-        in_specs=[pl.BlockSpec(memory_space=pltpu.VMEM)],
-        out_specs=pl.BlockSpec(memory_space=pltpu.VMEM),
+        kernel,
+        out_shape=jax.ShapeDtypeStruct(out, jnp.bfloat16),
+        in_specs=[vmem] * len(operands),
+        out_specs=vmem,
         scratch_shapes=[
+            pltpu.VMEM(operands[0].shape, jnp.bfloat16),
             pltpu.VMEM((rank, rank), jnp.float32),
             pltpu.VMEM((rank, rank), jnp.float32),
+            *more,
         ],
-        compiler_params=pltpu.CompilerParams(vmem_limit_bytes=48 << 20),
+        compiler_params=pltpu.CompilerParams(vmem_limit_bytes=30 << 20),
         cost_estimate=pl.CostEstimate(
-            flops=40_000_000_000, bytes_accessed=4 << 20, transcendentals=0
+            flops=20_000_000_000, bytes_accessed=8 << 20, transcendentals=0
         ),
-        name="orthonormal",
-    )(cluster_rows)
+        name=name,
+    )(*operands)
 
 
 CHUNKS = 4
+AHEAD = 2
 TILE = (16, 128)
 
 
 def exchange_kernel(
-    part, same, out, heard, pairs, met, own, tiles, tiles32, mixed32, mixed,
+    up, right, same, out, part, heard, pairs, met, own, tiles, tiles32, mixed32, mixed,
     first_sent, first_got, second_sent, second_got, out_sent, out_got, back_sent, back_got,
     share_sent, share_got,
 ):
@@ -166,6 +205,15 @@
     for other in (near, far):
         pl.semaphore_signal(barrier, inc=1, device_id=(me, other), device_id_type=MESH)
     lax.fori_loop(1, experts, greet, 0)
+
+    def multiply(i, carry):
+        rows = pl.ds(pl.multiple_of(i * block, block), block)
+        part[rows, :] = jnp.dot(
+            up[rows, :], right[...], preferred_element_type=jnp.float32
+        ).astype(jnp.bfloat16)
+        return carry
+
+    lax.fori_loop(0, n_token, multiply, 0)
     pl.semaphore_wait(barrier, experts + 1)
 
     def first(chunk, side, slot):
@@ -182,11 +230,10 @@
             second_sent.at[side, chunk], second_got.at[side, chunk], (me, (far, near)[side]),
         )
 
-    def start_first(chunk, carry):
+    def start_first(chunk):
         for side in range(2):
             for slot in (1, 0):
                 first(chunk, side, slot).start()
-        return carry
 
     def start_second(chunk):
         for side in range(2):
@@ -226,26 +273,6 @@
 
         lax.fori_loop(0, count, one, 0)
 
-    lax.fori_loop(0, CHUNKS, start_first, 0)
-    start_second(0)
-
-    def along(chunk, carry):
-        start_second(chunk)
-        scatter(chunk - 1)
-        return carry
-
-    lax.fori_loop(1, CHUNKS, along, 0)
-    scatter(CHUNKS - 1)
-
-    pltpu.make_async_copy(tiles, tiles, out_got).wait()
-    tiles32[...] = tiles[...].reshape(tiles32.shape).astype(jnp.float32)
-    for r in range(tile_rows):
-        every = pl.ds(r, experts, stride=tile_rows)
-        mixed32[every, :] = jnp.dot(
-            same[...], tiles32[every, :].astype(jnp.bfloat16), preferred_element_type=jnp.float32
-        )
-    mixed[...] = mixed32[...].astype(jnp.bfloat16).reshape(mixed.shape)
-
     my_chunk, my_deep, my_y = place(me)
     my_rows, my_cols = tile_at(t * block, my_chunk, my_deep, my_y)
 
@@ -256,8 +283,40 @@
         ).start()
         return carry
 
-    pltpu.make_async_copy(mixed.at[me], out.at[my_rows, my_cols], back_got.at[my_chunk]).start()
-    lax.fori_loop(1, experts, give, 0)
+    def give_back():
+        pltpu.make_async_copy(tiles, tiles, out_got).wait()
+        tiles32[...] = tiles[...].reshape(tiles32.shape).astype(jnp.float32)
+        for r in range(tile_rows):
+            every = pl.ds(r, experts, stride=tile_rows)
+            mixed32[every, :] = jnp.dot(
+                same[...],
+                tiles32[every, :].astype(jnp.bfloat16),
+                preferred_element_type=jnp.float32,
+            )
+        mixed[...] = mixed32[...].astype(jnp.bfloat16).reshape(mixed.shape)
+        pltpu.make_async_copy(mixed.at[me], out.at[my_rows, my_cols], back_got.at[my_chunk]).start()
+        lax.fori_loop(1, experts, give, 0)
+
+    for chunk in range(AHEAD):
+        start_first(chunk)
+
+    def along(chunk, carry):
+        @pl.when(chunk < CHUNKS)
+        def _():
+            start_second(chunk)
+
+        @pl.when(chunk + AHEAD < CHUNKS)
+        def _():
+            start_first(chunk + AHEAD)
+
+        @pl.when(chunk > 0)
+        def _():
+            scatter(chunk - 1)
+
+        return carry
+
+    lax.fori_loop(0, CHUNKS + 1, along, 0)
+    give_back()
 
     def share(chunk, kind):
         owner = (t, t, near, far)[kind]
@@ -305,8 +364,8 @@
     pltpu.make_async_copy(most, most, back_sent).wait()
 
 
-def exchange(partial_term, same):
-    rows, rank = partial_term.shape
+def exchange(up, right, same):
+    rows, rank = up.shape[0], right.shape[1]
     experts, n_token = lax.axis_size("expert"), lax.axis_size("token")
     block, half = rows // n_token, rank // 2
     step = block // CHUNKS
@@ -316,9 +375,10 @@
     return pl.pallas_call(
         exchange_kernel,
         out_shape=jax.ShapeDtypeStruct((rows, rank), jnp.bfloat16),
-        in_specs=[vmem, vmem],
+        in_specs=[vmem, vmem, vmem],
         out_specs=vmem,
         scratch_shapes=[
+            pltpu.VMEM((rows, rank), jnp.bfloat16),
             pltpu.VMEM((2, CHUNKS, 2, step, half), jnp.bfloat16),
             pltpu.VMEM((2, CHUNKS, step, half), jnp.bfloat16),
             pltpu.VMEM((2, CHUNKS, step, half), jnp.bfloat16),
@@ -331,48 +391,34 @@
             dma, dma, dma, dma((CHUNKS,)), dma((4, CHUNKS)), dma((4, CHUNKS)),
         ],
         compiler_params=pltpu.CompilerParams(
-            collective_id=0, has_side_effects=True, vmem_limit_bytes=40 << 20
+            collective_id=0, has_side_effects=True, vmem_limit_bytes=20 << 20
         ),
         cost_estimate=pl.CostEstimate(
             flops=60_000_000_000, bytes_accessed=8 << 20, transcendentals=0
         ),
         name="exchange",
-    )(partial_term, same)
-
-
-def new_basis(partial_term, same):
-    return orthonormal(exchange(partial_term, same))
+    )(up, right, same)
 
 
 def per_device(tokens, routes, assign, gate_weight, up_weight, sketch):
-    expert_count = lax.axis_size("expert")
-    gate_local = gate_weight[0]
-    up_local = up_weight[0]
+    gate, up = gate_weight[0], up_weight[0]
+    columns, rank = up.shape[1], sketch.shape[2]
     same = (assign[None, :] == assign[:, None]).astype(jnp.bfloat16)
-    partial_term = jnp.dot(up_local, sketch[0], preferred_element_type=jnp.float32).astype(
-        jnp.bfloat16
-    )
-    basis = new_basis(partial_term, same)
-    projected = lax.dot_general(
-        up_local, basis, (((0,), (0,)), ((), ())), preferred_element_type=jnp.float32
-    ).astype(jnp.bfloat16)
-    partial_term = jnp.dot(up_local, projected, preferred_element_type=jnp.float32).astype(
-        jnp.bfloat16
-    )
-    basis = new_basis(partial_term, same)
-    shard_rows = tokens.shape[0]
-    capacity = max(2, 2 * shard_rows * routes.shape[1] // expert_count)
-    outgoing = place_tokens(tokens, routes, expert_count, capacity)
-    arrived = lax.all_to_all(outgoing, "expert", split_axis=0, concat_axis=0, tiled=True)
-    slots_in = lax.all_gather(arrived, "token", axis=0, tiled=True)
-    slots_in = slots_in.reshape(-1, tokens.shape[1])
-    gate_value = jnp.dot(slots_in, gate_local, preferred_element_type=jnp.float32)
-    on_basis = jnp.dot(slots_in, basis, preferred_element_type=jnp.float32).astype(jnp.bfloat16)
-    coefficient = lax.dot_general(
-        basis, up_local, (((0,), (0,)), ((), ())), preferred_element_type=jnp.float32
-    ).astype(jnp.bfloat16)
-    merged = jnp.dot(on_basis, coefficient, preferred_element_type=jnp.float32)
-    hidden = (jax.nn.silu(gate_value) * merged).astype(jnp.bfloat16)
+    rows = exchange(up, sketch[0], same)
+    projected = with_basis(gram_kernel, "gram", (columns, rank), rank, [], rows, up)
+    slots_in = lax.all_gather(own_slots(tokens, routes), "token", axis=0, tiled=True)
+    rows = exchange(up, projected, same)
+    hidden = with_basis(
+        hidden_kernel,
+        "hidden",
+        (slots_in.shape[0], columns),
+        rank,
+        [pltpu.VMEM((rank, columns), jnp.bfloat16)],
+        rows,
+        up,
+        gate,
+        slots_in,
+    )
     return hidden[None]
 
 

time: 333 us -> 353 us (1.060)
  waiting for transfers between devices: 0.04 us -> 65.9 us
  starting transfers between devices: 20.8 us -> 0.04 us
  matrix products: 22 us -> 6.19 us
  Pallas kernels: 255 us -> 245 us
  other arithmetic: 0.4 us -> 4.53 us
    all_gather x1 -> x2, waiting for transfers between devices: 0.02 us -> 65.8 us  [the longest x1 65.8 us: own_slots(): lax.all_gather(jnp.concatenate([tokens, marked], axis=1), 'expert', axis=...]
    all_to_all x1 -> x0, starting transfers between devices: 20.6 us -> none  [per_device(): lax.all_to_all(outgoing, 'expert', split_axis=0, concat_axis=0, tiled=True)]
    dot_general x6 -> x1, matrix products: 22 us -> 6.19 us  [own_slots(): picked = jnp.dot(select, every, preferred_element_type=jnp.float32)]
    pallas_call x2, Pallas kernels: 213 us -> 199 us  [exchange(): pl.pallas_call(exchange_kernel, out_shape=jax.ShapeDtypeStruct((rows, ran...]
    reshape x2 -> x0, local copies, waits for them, and re-layouts: 8.86 us -> none  [the longest x1 7.34 us: per_device(): slots_in = slots_in.reshape(-1, tokens.shape[1])]
    unnamed x17 -> x19, local copies, waits for them, and re-layouts: 6.17 us -> 11.2 us
    pallas_call x2, Pallas kernels: 42.3 us -> 46.4 us  [with_basis(): pl.pallas_call(kernel, out_shape=jax.ShapeDtypeStruct(out, jnp.bfloat16),...]
  transfers between devices with their start and end apart: 2 -> 2, of which waited for: 0 -> 1; matrix products, arithmetic and copies ran while one was open for 2% -> 0% of each run, Pallas kernels for 78% -> 65%
where the time goes in v3:
time: 353 us; the launch traced here: 348 us
  Pallas kernels  245 us (69%)
  waiting for transfers between devices  65.9 us (19%)
  between operations  13.5 us (4%)
  local copies, waits for them, and re-layouts  12.9 us (4%)
  matrix products  6.19 us (2%)
  other arithmetic  4.53 us (1%)
    pallas_call x2, Pallas kernels, exchange(): pl.pallas_call(exchange_kernel, out_shape=jax.ShapeDtypeStruct((rows, ran...  199 us
    all_gather x1, waiting for transfers between devices, own_slots(): lax.all_gather(jnp.concatenate([tokens, marked], axis=1), 'expert', axis=...  65.8 us
    pallas_call x2, Pallas kernels, with_basis(): pl.pallas_call(kernel, out_shape=jax.ShapeDtypeStruct(out, jnp.bfloat16),...  46.4 us
    unnamed x19, local copies, waits for them, and re-layouts  11.2 us
  transfers between devices with their start and end apart: 2, of which 1 were waited for; matrix products, arithmetic and copies ran while one was open for 0% of the time, Pallas kernels for 65%

profile of v3, /device:TPU:1, one launch (start us, length us, event | category | flops | bytes accessed | tf_op | source)
XLA Modules:
  0.0 347.9 jit_solution(14157832987590606840)
XLA Ops:
  6.5 0.7 convert_element_type.17
  7.3 1.5 fusion.3
  8.9 0.8 compare_convert_fusion.same
  9.7 1.4 copy-done.1
  11.1 1.0 copy-done.4
  12.1 99.6 %exchange.2.rows_ref = bf16[2048,512]{1,0:T(8,128)(2,1)S(1)} custom-call(bf16[2048,384]{1,0:T(8,128)(2,1)S(1)} %bitcast.5, bf16[384,512]{1,0:T(8,128)(2,1)S(1)} %bitcast.10, bf16[128,128]{1,0:T(8,128)(2,1)S(1)} %compare_convert_fusion.same), custom_call_target="tpu_custom_call" | custom-call | flops 60000002048 | bytes 8388608 | tf_op jit(solution)/shard_map/exchange/pallas_call | solution.py:375
  111.8 1.4 copy-done.7
  113.1 65.8 %all-gather.3.cloned.1.call-done = bf16[2048,2176]{1,0:T(8,128)(2,1)} async-done(((bf16[16,2176]{1,0:T(8,128)(2,1)}), bf16[2048,2176]{1,0:T(8,128)(2,1)}) %all-gather.3.cloned.1.call-update) | async-done | bytes 8912912 | tf_op jit(solution)/shard_map/all_gather | solution.py:27
  178.9 1.4 compare_reduce_fusion
  180.3 0.1 and.23
  180.5 0.1 convert_reduce_fusion
  180.7 0.1 copy.11
  180.8 0.1 lt.35
  180.9 0.1 copy.12
  181.1 6.2 %fusion = bf16[256,2176]{1,0:T(8,128)(2,1)S(1)} fusion(bf16[2048,2176]{1,0:T(8,128)(2,1)} %all-gather.3.cloned.1.call-done, s32[2048]{0:T(1024)S(1)} %and_select_fusion), kind=kOutput, calls=%fused_computation.2 | convolution fusion | flops 2282225664 | bytes 10035200 | tf_op jit(solution)/shard_map/dot_general | solution.py:38
  187.3 1.1 slice.13
  188.4 0.6 copy-done.2
  189.1 1.6 copy-done.8
  190.7 26.3 %gram.1.right = bf16[384,512]{1,0:T(8,128)(2,1)S(1)} custom-call(bf16[2048,512]{1,0:T(8,128)(2,1)S(1)} %copy-done.8, bf16[2048,384]{1,0:T(8,128)(2,1)S(1)} %bitcast.6), custom_call_target="tpu_custom_call" | custom-call | flops 20000000000 | bytes 8388608 | tf_op jit(solution)/shard_map/gram/pallas_call | solution.py:138
  217.0 98.9 %exchange.3.rows_ref = bf16[2048,512]{1,0:T(8,128)(2,1)S(1)} custom-call(bf16[2048,384]{1,0:T(8,128)(2,1)S(1)} %bitcast.7, bf16[384,512]{1,0:T(8,128)(2,1)S(1)} %gram.1.right, bf16[128,128]{1,0:T(8,128)(2,1)S(1)} %compare_convert_fusion.same), custom_call_target="tpu_custom_call" | custom-call | flops 60000002048 | bytes 8388608 | tf_op jit(solution)/shard_map/exchange/pallas_call | solution.py:375
  315.9 1.3 copy-done.5
  317.2 2.2 copy-done
  319.4 1.6 copy-done.6
  321.0 20.1 %hidden.1 = bf16[1024,384]{1,0:T(8,128)(2,1)} custom-call(bf16[2048,512]{1,0:T(8,128)(2,1)S(1)} %copy-done.6, bf16[2048,384]{1,0:T(8,128)(2,1)S(1)} %bitcast.8, bf16[2048,384]{1,0:T(8,128)(2,1)S(1)} %bitcast.9, bf16[1024,2048]{1,0:T(8,128)(2,1)S(1)} %copy-done), custom_call_target="tpu_custom_call" | custom-call | flops 20000000000 | bytes 8388608 | tf_op jit(solution)/shard_map/hidden/pallas_call | solution.py:138
  (23 shorter events, 0.4 us)
Async XLA Ops:
  6.5 172.4 %all-gather.3.cloned.1.call-start = ((), (), s32[]{:S(2)}) async-start(), calls=%async_computation | async-start | bytes 8982528 | tf_op jit(solution)/shard_map/all_gather | solution.py:27
  8.8 308.4 %all-gather.5.cloned.1.call-start = ((), (), s32[]{:S(2)}) async-start(), calls=%async_computation.1 | async-start | bytes 5242880 | tf_op jit(solution)/shard_map/all_gather | solution.py:409
  9.7 1.4 copy-start.1
  11.1 1.0 copy-start.4
  111.7 1.4 copy-start.7
  187.3 1.8 copy-start.2
  189.1 1.6 copy-start.8
  216.9 100.2 %copy-start.3 = (bf16[1,2048,384]{2,1,0:T(8,128)(2,1)S(1)}, bf16[1,2048,384]{2,1,0:T(8,128)(2,1)}, u32[]{:S(2)}) copy-start(bf16[1,2048,384]{2,1,0:T(8,128)(2,1)} %param.9) | copy-start | bytes 4718596
  315.9 1.3 copy-start.5
  317.2 2.2 copy-start
  319.4 1.6 copy-start.6
Sparse Core Ops, SparseCore 0:
  10.4 168.4 all-gather.2
  188.6 55.3 all-gather.4

commit v4 on v3

--- a/solution.py
+++ b/solution.py
@@ -16,27 +16,63 @@
 MOST = 60
 OVER_ROWS = (((0,), (0,)), ((), ()))
 SLOT_ROWS = 256
-
-
-def own_slots(tokens, routes):
+PLANE = 8
+
+
+def line_tokens(tokens, routes):
     expert_count = lax.axis_size("expert")
-    rows, width = tokens.shape
+    planes = expert_count // PLANE
     top = routes.shape[1]
-    capacity = max(2, 2 * rows * top // expert_count)
     marked = jnp.pad(routes.astype(jnp.bfloat16), ((0, 0), (0, 128 - top)), constant_values=-1)
-    every = lax.all_gather(
-        jnp.concatenate([tokens, marked], axis=1), "expert", axis=0, tiled=True
-    )
-    me = lax.axis_index("expert").astype(jnp.bfloat16)
-    named = jnp.any(every[:, width:] == me, axis=1).reshape(expert_count, rows)
-    before = jnp.arange(rows)[:, None] < jnp.arange(rows)[None, :]
-    slot = jnp.sum((named[:, :, None] & before[None]).astype(jnp.int32), axis=1)
-    target = jnp.arange(expert_count, dtype=jnp.int32)[:, None] * capacity + slot
-    target = jnp.where(named & (slot < capacity), target, -1).reshape(1, -1)
-    place = jnp.arange(expert_count * capacity, dtype=jnp.int32)[:, None]
-    select = (place == target).astype(jnp.bfloat16)
-    picked = jnp.dot(select, every, preferred_element_type=jnp.float32)
-    return picked[:, :width].astype(jnp.bfloat16)
+    return lax.all_gather(
+        jnp.concatenate([tokens, marked], axis=1),
+        "expert",
+        axis=0,
+        tiled=True,
+        axis_index_groups=[[z * PLANE + i for z in range(planes)] for i in range(PLANE)],
+    )
+
+
+def picked_slots(every, rows, width, capacity):
+    planes = every.shape[0] // rows
+    me = lax.axis_index("expert")
+    spot = me % PLANE
+    turn = jnp.arange(PLANE, dtype=jnp.int32)
+    to = (me - spot + (spot + turn) % PLANE).astype(jnp.bfloat16)
+    named = jnp.any(every[None, :, width:] == to[:, None, None], axis=2)
+    n = jnp.arange(planes * rows, dtype=jnp.int32)
+    before = (n[:, None] < n[None, :]) & (n[:, None] // rows == n[None, :] // rows)
+    slot = jnp.dot(
+        named.astype(jnp.bfloat16), before.astype(jnp.bfloat16), preferred_element_type=jnp.float32
+    ).astype(jnp.int32)
+    target = jnp.where(named & (slot < capacity), n[None, :] // rows * capacity + slot, -1)
+    place = jnp.arange(planes * capacity, dtype=jnp.int32)
+    select = (place[None, :, None] == target[:, None, :]).astype(jnp.bfloat16)
+    picked = jnp.dot(
+        select.reshape(-1, planes * rows), every[:, :width], preferred_element_type=jnp.float32
+    ).astype(jnp.bfloat16)
+    return picked.reshape(PLANE, planes * capacity, width)
+
+
+def plane_slots(picked):
+    expert_count = lax.axis_size("expert")
+    came = [picked[0]]
+    for i in range(1, PLANE):
+        pairs = [(e, e - e % PLANE + (e % PLANE + i) % PLANE) for e in range(expert_count)]
+        came.append(lax.ppermute(picked[i], "expert", pairs))
+    return came
+
+
+def ordered_slots(came, capacity):
+    planes = lax.axis_size("expert") // PLANE
+    spot = lax.axis_index("expert") % PLANE
+    source = jnp.arange(PLANE * planes * capacity, dtype=jnp.int32)
+    sender = (spot + PLANE - source // (planes * capacity)) % PLANE
+    z, s = source // capacity % planes, source % capacity
+    order = (source[:, None] == ((z * PLANE + sender) * capacity + s)[None, :]).astype(jnp.bfloat16)
+    return jnp.dot(
+        order, jnp.concatenate(came, axis=0), preferred_element_type=jnp.float32
+    ).astype(jnp.bfloat16)
 
 
 def dot16(a, b):
@@ -404,9 +440,17 @@
     gate, up = gate_weight[0], up_weight[0]
     columns, rank = up.shape[1], sketch.shape[2]
     same = (assign[None, :] == assign[:, None]).astype(jnp.bfloat16)
+    capacity = max(2, 2 * tokens.shape[0] * routes.shape[1] // lax.axis_size("expert"))
+    every = line_tokens(tokens, routes)
     rows = exchange(up, sketch[0], same)
+    every, rows = lax.optimization_barrier((every, rows))
+    picked = picked_slots(every, *tokens.shape, capacity)
+    picked, rows = lax.optimization_barrier((picked, rows))
+    came = plane_slots(picked)
     projected = with_basis(gram_kernel, "gram", (columns, rank), rank, [], rows, up)
-    slots_in = lax.all_gather(own_slots(tokens, routes), "token", axis=0, tiled=True)
+    came, projected = lax.optimization_barrier((came, projected))
+    slots, projected = lax.optimization_barrier((ordered_slots(came, capacity), projected))
+    slots_in = lax.all_gather(slots, "token", axis=0, tiled=True)
     rows = exchange(up, projected, same)
     hidden = with_basis(
         hidden_kernel,

time: 353 us -> 303 us (0.86)
  the two profiles are of different devices: /device:TPU:1 before, /device:TPU:34 now
where the time goes in v4:
time: 303 us; the launch traced here: 302 us
  Pallas kernels  251 us (83%)
  starting transfers between devices  16.9 us (6%)
  between operations  13.7 us (5%)
  local copies, waits for them, and re-layouts  13.4 us (4%)
  other arithmetic  3.54 us (1%)
  matrix products  3.44 us (1%)
    pallas_call x2, Pallas kernels, exchange(): pl.pallas_call(exchange_kernel, out_shape=jax.ShapeDtypeStruct((rows, ran...  201 us
    pallas_call x2, Pallas kernels, with_basis(): pl.pallas_call(kernel, out_shape=jax.ShapeDtypeStruct(out, jnp.bfloat16),...  50.6 us
    ppermute x7, starting transfers between devices, plane_slots(): came.append(lax.ppermute(picked[i], 'expert', pairs))  16.9 us
    unnamed x30, local copies, waits for them, and re-layouts  12.3 us
  transfers between devices with their start and end apart: 9, of which 0 were waited for; matrix products, arithmetic and copies ran while one was open for 0% of the time, Pallas kernels for 75%

profile of v4, /device:TPU:34, one launch (start us, length us, event | category | flops | bytes accessed | tf_op | source)
XLA Modules:
  0.0 302.2 jit_solution(5161015834947175215)
XLA Ops:
  7.3 1.5 fusion.8
  8.9 0.8 compare_convert_fusion.same
  9.7 1.4 copy-done.1
  11.1 1.0 copy-done.4
  12.1 102.1 %exchange.2.rows_ref = bf16[2048,512]{1,0:T(8,128)(2,1)S(1)} custom-call(bf16[2048,384]{1,0:T(8,128)(2,1)S(1)} %bitcast.26, bf16[384,512]{1,0:T(8,128)(2,1)S(1)} %bitcast.31, bf16[128,128]{1,0:T(8,128)(2,1)S(1)} %compare_convert_fusion.same), custom_call_target="tpu_custom_call" | custom-call | flops 60000002048 | bytes 8388608 | tf_op jit(solution)/shard_map/exchange/pallas_call | solution.py:411
  114.2 1.3 copy-done.7
  115.7 0.8 slice.30
  117.3 1.8 convolution_convert_fusion.1
  119.2 0.8 collective-permute-start.6
  120.0 4.1 %collective-permute-start.5 = (bf16[32,2048]{1,0:T(8,128)(2,1)S(1)}, bf16[32,2048]{1,0:T(8,128)(2,1)S(1)}, u32[]{:S(2)}, u32[]{:S(2)}) collective-permute-start(bf16[32,2048]{1,0:T(8,128)(2,1)S(1)} %get-tuple-element.36), channel_id=1, source_target_pairs={{0,24},{4,28},{8,0},{12,4},{16,8},{20,12},{24,16},{28,20},{32,56},... | collective-permute-start | bytes 393224 | tf_op jit(solution)/shard_map/ppermute | solution.py:62
  124.1 1.9 collective-permute-start.4
  126.1 5.2 %collective-permute-start.3 = (bf16[32,2048]{1,0:T(8,128)(2,1)S(1)}, bf16[32,2048]{1,0:T(8,128)(2,1)S(1)}, u32[]{:S(2)}, u32[]{:S(2)}) collective-permute-start(bf16[32,2048]{1,0:T(8,128)(2,1)S(1)} %get-tuple-element.38), channel_id=1, source_target_pairs={{0,16},{4,20},{8,24},{12,28},{16,0},{20,4},{24,8},{28,12},{32,48},... | collective-permute-start | bytes 393224 | tf_op jit(solution)/shard_map/ppermute | solution.py:62
  131.3 1.9 collective-permute-start.2
  133.2 1.9 collective-permute-start.1
  135.2 1.0 collective-permute-start
  136.2 1.6 copy-done.8
  137.8 26.3 %gram.1.right = bf16[384,512]{1,0:T(8,128)(2,1)S(1)} custom-call(bf16[2048,512]{1,0:T(8,128)(2,1)S(1)} %copy-done.8, bf16[2048,384]{1,0:T(8,128)(2,1)S(1)} %bitcast.27), custom_call_target="tpu_custom_call" | custom-call | flops 20000000000 | bytes 8388608 | tf_op jit(solution)/shard_map/gram/pallas_call | solution.py:174
  165.0 1.4 convolution_convert_fusion
  166.4 1.0 copy-done.10
  167.4 98.5 %exchange.3.rows_ref = bf16[2048,512]{1,0:T(8,128)(2,1)S(1)} custom-call(bf16[2048,384]{1,0:T(8,128)(2,1)S(1)} %bitcast.28, bf16[384,512]{1,0:T(8,128)(2,1)S(1)} %copy-done.10, bf16[128,128]{1,0:T(8,128)(2,1)S(1)} %compare_convert_fusion.same), custom_call_target="tpu_custom_call" | custom-call | flops 60000002048 | bytes 8388608 | tf_op jit(solution)/shard_map/exchange/pallas_call | solution.py:411
  266.0 1.3 copy-done.5
  267.3 2.2 copy-done
  269.5 1.6 copy-done.6
  271.1 24.3 %hidden.1 = bf16[1024,384]{1,0:T(8,128)(2,1)} custom-call(bf16[2048,512]{1,0:T(8,128)(2,1)S(1)} %copy-done.6, bf16[2048,384]{1,0:T(8,128)(2,1)S(1)} %bitcast.29, bf16[2048,384]{1,0:T(8,128)(2,1)S(1)} %bitcast.30, bf16[1024,2048]{1,0:T(8,128)(2,1)S(1)} %copy-done), custom_call_target="tpu_custom_call" | custom-call | flops 20000000000 | bytes 8388608 | tf_op jit(solution)/shard_map/hidden/pallas_call | solution.py:174
  (46 shorter events, 2.7 us)
Async XLA Ops:
  6.5 109.1 %all-gather.3.cloned.1.call-start = ((), (), s32[]{:S(2)}) async-start(), calls=%async_computation | async-start | bytes 1183744 | tf_op jit(solution)/shard_map/all_gather | solution.py:27
  8.8 258.5 %all-gather.5.cloned.1.call-start = ((), (), s32[]{:S(2)}) async-start(), calls=%async_computation.1 | async-start | bytes 5242880 | tf_op jit(solution)/shard_map/all_gather | solution.py:453
  9.7 1.4 copy-start.1
  11.1 1.0 copy-start.4
  114.2 1.3 copy-start.7
  117.3 18.9 %copy-start.2 = (bf16[1,2048,384]{2,1,0:T(8,128)(2,1)S(1)}, bf16[1,2048,384]{2,1,0:T(8,128)(2,1)}, u32[]{:S(2)}) copy-start(bf16[1,2048,384]{2,1,0:T(8,128)(2,1)} %param.10) | copy-start | bytes 4718596
  119.2 14.0 %collective-permute-start.6 = (bf16[32,2048]{1,0:T(8,128)(2,1)S(1)}, bf16[32,2048]{1,0:T(8,128)(2,1)S(1)}, u32[]{:S(2)}, u32[]{:S(2)}) collective-permute-start(bf16[32,2048]{1,0:T(8,128)(2,1)S(1)} %get-tuple-element.35), channel_id=1, source_target_pairs={{0,28},{4,0},{8,4},{12,8},{16,12},{20,16},{24,20},{28,24},{32,60},... | collective-permute-start | bytes 393224 | tf_op jit(solution)/shard_map/ppermute | solution.py:62
  120.0 15.2 %collective-permute-start.5 = (bf16[32,2048]{1,0:T(8,128)(2,1)S(1)}, bf16[32,2048]{1,0:T(8,128)(2,1)S(1)}, u32[]{:S(2)}, u32[]{:S(2)}) collective-permute-start(bf16[32,2048]{1,0:T(8,128)(2,1)S(1)} %get-tuple-element.36), channel_id=1, source_target_pairs={{0,24},{4,28},{8,0},{12,4},{16,8},{20,12},{24,16},{28,20},{32,56},... | collective-permute-start | bytes 393224 | tf_op jit(solution)/shard_map/ppermute | solution.py:62
  124.1 40.6 %collective-permute-start.4 = (bf16[32,2048]{1,0:T(8,128)(2,1)S(1)}, bf16[32,2048]{1,0:T(8,128)(2,1)S(1)}, u32[]{:S(2)}, u32[]{:S(2)}) collective-permute-start(bf16[32,2048]{1,0:T(8,128)(2,1)S(1)} %get-tuple-element.37), channel_id=1, source_target_pairs={{0,20},{4,24},{8,28},{12,0},{16,4},{20,8},{24,12},{28,16},{32,52},... | collective-permute-start | bytes 393224 | tf_op jit(solution)/shard_map/ppermute | solution.py:62
  126.1 38.7 %collective-permute-start.3 = (bf16[32,2048]{1,0:T(8,128)(2,1)S(1)}, bf16[32,2048]{1,0:T(8,128)(2,1)S(1)}, u32[]{:S(2)}, u32[]{:S(2)}) collective-permute-start(bf16[32,2048]{1,0:T(8,128)(2,1)S(1)} %get-tuple-element.38), channel_id=1, source_target_pairs={{0,16},{4,20},{8,24},{12,28},{16,0},{20,4},{24,8},{28,12},{32,48},... | collective-permute-start | bytes 393224 | tf_op jit(solution)/shard_map/ppermute | solution.py:62
  131.3 33.5 %collective-permute-start.2 = (bf16[32,2048]{1,0:T(8,128)(2,1)S(1)}, bf16[32,2048]{1,0:T(8,128)(2,1)S(1)}, u32[]{:S(2)}, u32[]{:S(2)}) collective-permute-start(bf16[32,2048]{1,0:T(8,128)(2,1)S(1)} %get-tuple-element.39), channel_id=1, source_target_pairs={{0,12},{4,16},{8,20},{12,24},{16,28},{20,0},{24,4},{28,8},{32,44},... | collective-permute-start | bytes 393224 | tf_op jit(solution)/shard_map/ppermute | solution.py:62
  133.2 31.5 %collective-permute-start.1 = (bf16[32,2048]{1,0:T(8,128)(2,1)S(1)}, bf16[32,2048]{1,0:T(8,128)(2,1)S(1)}, u32[]{:S(2)}, u32[]{:S(2)}) collective-permute-start(bf16[32,2048]{1,0:T(8,128)(2,1)S(1)} %get-tuple-element.40), channel_id=1, source_target_pairs={{0,8},{4,12},{8,16},{12,20},{16,24},{20,28},{24,0},{28,4},{32,40},... | collective-permute-start | bytes 393224 | tf_op jit(solution)/shard_map/ppermute | solution.py:62
  135.2 29.6 %collective-permute-start = (bf16[32,2048]{1,0:T(8,128)(2,1)S(1)}, bf16[32,2048]{1,0:T(8,128)(2,1)S(1)}, u32[]{:S(2)}, u32[]{:S(2)}) collective-permute-start(bf16[32,2048]{1,0:T(8,128)(2,1)S(1)} %get-tuple-element.41), channel_id=1, source_target_pairs={{0,4},{4,8},{8,12},{12,16},{16,20},{20,24},{24,28},{28,0},{32,36},... | collective-permute-start | bytes 393224 | tf_op jit(solution)/shard_map/ppermute | solution.py:62
  136.2 1.6 copy-start.8
  164.0 0.7 copy-start.9
  166.4 1.0 copy-start.10
  167.4 99.9 %copy-start.3 = (bf16[1,2048,384]{2,1,0:T(8,128)(2,1)S(1)}, bf16[1,2048,384]{2,1,0:T(8,128)(2,1)}, u32[]{:S(2)}) copy-start(bf16[1,2048,384]{2,1,0:T(8,128)(2,1)} %param.9) | copy-start | bytes 4718596
  266.0 1.3 copy-start.5
  267.3 2.2 copy-start
  269.5 1.6 copy-start.6
Sparse Core Ops, SparseCore 0:
  9.4 96.2 all-gather.2
  166.5 67.8 all-gather.4

commit v5 on v4

--- a/solution.py
+++ b/solution.py
@@ -16,7 +16,9 @@
 MOST = 60
 OVER_ROWS = (((0,), (0,)), ((), ()))
 SLOT_ROWS = 256
-PLANE = 8
+CORES = 2
+LINE = 4
+PLANE = LINE * CORES
 
 
 def line_tokens(tokens, routes):
@@ -38,7 +40,8 @@
     me = lax.axis_index("expert")
     spot = me % PLANE
     turn = jnp.arange(PLANE, dtype=jnp.int32)
-    to = (me - spot + (spot + turn) % PLANE).astype(jnp.bfloat16)
+    to = me - spot + (spot + turn % LINE * CORES) % PLANE
+    to = (to + turn // LINE * (1 - 2 * (me % CORES))).astype(jnp.bfloat16)
     named = jnp.any(every[None, :, width:] == to[:, None, None], axis=2)
     n = jnp.arange(planes * rows, dtype=jnp.int32)
     before = (n[:, None] < n[None, :]) & (n[:, None] // rows == n[None, :] // rows)
@@ -51,15 +54,17 @@
     picked = jnp.dot(
         select.reshape(-1, planes * rows), every[:, :width], preferred_element_type=jnp.float32
     ).astype(jnp.bfloat16)
-    return picked.reshape(PLANE, planes * capacity, width)
+    return picked.reshape(CORES, LINE, planes * capacity, width)
 
 
 def plane_slots(picked):
-    expert_count = lax.axis_size("expert")
-    came = [picked[0]]
-    for i in range(1, PLANE):
-        pairs = [(e, e - e % PLANE + (e % PLANE + i) % PLANE) for e in range(expert_count)]
-        came.append(lax.ppermute(picked[i], "expert", pairs))
+    everyone = range(lax.axis_size("expert"))
+    mates = [(e, e + 1 - 2 * (e % CORES)) for e in everyone]
+    both = jnp.stack([picked[0], lax.ppermute(picked[1], "expert", mates)], axis=1)
+    came = [both[0]]
+    for i in range(1, LINE):
+        pairs = [(e, e - e % PLANE + (e % PLANE + i * CORES) % PLANE) for e in everyone]
+        came.append(lax.ppermute(both[i], "expert", pairs))
     return came
 
 
@@ -67,11 +72,13 @@
     planes = lax.axis_size("expert") // PLANE
     spot = lax.axis_index("expert") % PLANE
     source = jnp.arange(PLANE * planes * capacity, dtype=jnp.int32)
-    sender = (spot + PLANE - source // (planes * capacity)) % PLANE
+    step = source // (planes * capacity)
+    sender = (spot + PLANE - step // CORES * CORES) % PLANE
+    sender = sender + step % CORES * (1 - 2 * (spot % CORES))
     z, s = source // capacity % planes, source % capacity
     order = (source[:, None] == ((z * PLANE + sender) * capacity + s)[None, :]).astype(jnp.bfloat16)
     return jnp.dot(
-        order, jnp.concatenate(came, axis=0), preferred_element_type=jnp.float32
+        order, jnp.concatenate(came, axis=0).reshape(source.shape[0], -1), preferred_element_type=jnp.float32
     ).astype(jnp.bfloat16)
 
 
@@ -146,12 +153,17 @@
 
 
 def hidden_kernel(
-    rows_ref, up_ref, gate_ref, slots_ref, hidden_ref, basis_ref, gram_ref, x_ref, coefficient_ref
+    rows_ref, up_ref, gate_ref, slots_hbm, hidden_ref, basis_ref, gram_ref, x_ref, coefficient_ref,
+    slots_ref, loaded,
 ):
+    load = pltpu.make_async_copy(slots_hbm, slots_ref, loaded)
+    load.start()
     orthonormal(rows_ref, basis_ref, gram_ref, x_ref)
     coefficient_ref[...] = lax.dot_general(
         basis_ref[...], up_ref[...], OVER_ROWS, preferred_element_type=jnp.float32
     ).astype(jnp.bfloat16)
+
+    load.wait()
 
     def some(i, carry):
         these = pl.ds(pl.multiple_of(i * SLOT_ROWS, SLOT_ROWS), SLOT_ROWS)
@@ -169,12 +181,12 @@
     lax.fori_loop(0, slots_ref.shape[0] // SLOT_ROWS, some, 0)
 
 
-def with_basis(kernel, name, out, rank, more, *operands):
+def with_basis(kernel, name, out, rank, more, far, *operands):
     vmem = pl.BlockSpec(memory_space=pltpu.VMEM)
     return pl.pallas_call(
         kernel,
         out_shape=jax.ShapeDtypeStruct(out, jnp.bfloat16),
-        in_specs=[vmem] * len(operands),
+        in_specs=[vmem] * (len(operands) - far) + [pl.BlockSpec(memory_space=pl.ANY)] * far,
         out_specs=vmem,
         scratch_shapes=[
             pltpu.VMEM(operands[0].shape, jnp.bfloat16),
@@ -182,7 +194,7 @@
             pltpu.VMEM((rank, rank), jnp.float32),
             *more,
         ],
-        compiler_params=pltpu.CompilerParams(vmem_limit_bytes=30 << 20),
+        compiler_params=pltpu.CompilerParams(vmem_limit_bytes=(56 if far else 30) << 20),
         cost_estimate=pl.CostEstimate(
             flops=20_000_000_000, bytes_accessed=8 << 20, transcendentals=0
         ),
@@ -447,7 +459,7 @@
     picked = picked_slots(every, *tokens.shape, capacity)
     picked, rows = lax.optimization_barrier((picked, rows))
     came = plane_slots(picked)
-    projected = with_basis(gram_kernel, "gram", (columns, rank), rank, [], rows, up)
+    projected = with_basis(gram_kernel, "gram", (columns, rank), rank, [], 0, rows, up)
     came, projected = lax.optimization_barrier((came, projected))
     slots, projected = lax.optimization_barrier((ordered_slots(came, capacity), projected))
     slots_in = lax.all_gather(slots, "token", axis=0, tiled=True)
@@ -457,7 +469,12 @@
         "hidden",
         (slots_in.shape[0], columns),
         rank,
-        [pltpu.VMEM((rank, columns), jnp.bfloat16)],
+        [
+            pltpu.VMEM((rank, columns), jnp.bfloat16),
+            pltpu.VMEM(slots_in.shape, jnp.bfloat16),
+            pltpu.SemaphoreType.DMA,
+        ],
+        1,
         rows,
         up,
         gate,

time: 303 us -> 295 us (0.974)
  the two profiles are of different devices: /device:TPU:34 before, /device:TPU:1 now
where the time goes in v5:
time: 295 us; the launch traced here: 290 us
  Pallas kernels  247 us (84%)
  starting transfers between devices  14.3 us (5%)
  between operations  13.6 us (5%)
  local copies, waits for them, and re-layouts  6.2 us (2%)
  other arithmetic  3.78 us (1%)
  matrix products  3.35 us (1%)
    pallas_call x2, Pallas kernels, exchange(): pl.pallas_call(exchange_kernel, out_shape=jax.ShapeDtypeStruct((rows, ran...  198 us
    pallas_call x2, Pallas kernels, with_basis(): pl.pallas_call(kernel, out_shape=jax.ShapeDtypeStruct(out, jnp.bfloat16),...  48.7 us
    ppermute x3, starting transfers between devices, plane_slots(): came.append(lax.ppermute(both[i], 'expert', pairs))  10.1 us
  transfers between devices with their start and end apart: 6, of which 1 were waited for; matrix products, arithmetic and copies ran while one was open for 0% of the time, Pallas kernels for 77%

profile of v5, /device:TPU:1, one launch (start us, length us, event | category | flops | bytes accessed | tf_op | source)
XLA Modules:
  0.0 289.5 jit_solution(14027671310235180025)
XLA Ops:
  6.5 0.7 convert_element_type.28
  7.3 1.5 fusion.15
  8.9 0.8 compare_convert_fusion.same
  9.7 1.4 copy-done
  11.1 1.0 copy-done.2
  12.1 100.6 %exchange.2.rows_ref = bf16[2048,512]{1,0:T(8,128)(2,1)S(1)} custom-call(bf16[2048,384]{1,0:T(8,128)(2,1)S(1)} %bitcast.31, bf16[384,512]{1,0:T(8,128)(2,1)S(1)} %bitcast.34, bf16[128,128]{1,0:T(8,128)(2,1)S(1)} %compare_convert_fusion.same), custom_call_target="tpu_custom_call" | custom-call | flops 60000002048 | bytes 8388608 | tf_op jit(solution)/shard_map/exchange/pallas_call | solution.py:423
  112.7 1.3 copy-done.4
  114.2 0.8 slice.24
  115.0 0.4 compare_reduce_fusion
  115.4 0.2 add_select_fusion
  115.7 0.1 bitcast_compare_fusion
  115.8 1.7 convolution_convert_fusion.1
  117.5 0.1 slice_bitcast_fusion
  117.6 4.2 %collective-permute-start = (bf16[4,32,2048]{2,1,0:T(8,128)(2,1)S(1)}, bf16[4,32,2048]{2,1,0:T(8,128)(2,1)S(1)}, u32[]{:S(2)}, u32[]{:S(2)}) collective-permute-start(bf16[4,32,2048]{2,1,0:T(8,128)(2,1)S(1)} %get-tuple-element.31), channel_id=1, source_target_pairs={{0,4},{4,0},{8,12},{12,8},{16,20},{20,16},{24,28},{28,24},{32,36},... | collective-permute-start | bytes 1572872 | tf_op jit(solution)/shard_map/ppermute | solution.py:63
  121.8 1.5 collective-permute-done
  123.4 5.1 %collective-permute-start.3 = (bf16[2,32,2048]{2,1,0:T(8,128)(2,1)S(1)}, bf16[2,32,2048]{2,1,0:T(8,128)(2,1)S(1)}, u32[]{:S(2)}, u32[]{:S(2)}) collective-permute-start(bf16[2,32,2048]{2,1,0:T(8,128)(2,1)S(1)} %get-tuple-element.27), channel_id=1, source_target_pairs={{0,24},{4,28},{8,0},{12,4},{16,8},{20,12},{24,16},{28,20},{32,56},... | collective-permute-start | bytes 786440 | tf_op jit(solution)/shard_map/ppermute | solution.py:67
  128.5 1.9 collective-permute-start.1
  130.4 3.1 %collective-permute-start.2 = (bf16[2,32,2048]{2,1,0:T(8,128)(2,1)S(1)}, bf16[2,32,2048]{2,1,0:T(8,128)(2,1)S(1)}, u32[]{:S(2)}, u32[]{:S(2)}) collective-permute-start(bf16[2,32,2048]{2,1,0:T(8,128)(2,1)S(1)} %get-tuple-element.30), channel_id=1, source_target_pairs={{0,16},{4,20},{8,24},{12,28},{16,0},{20,4},{24,8},{28,12},{32,48},... | collective-permute-start | bytes 786440 | tf_op jit(solution)/shard_map/ppermute | solution.py:67
  133.5 26.3 %gram.1.right = bf16[384,512]{1,0:T(8,128)(2,1)S(1)} custom-call(bf16[2048,512]{1,0:T(8,128)(2,1)S(1)} %copy-done.5, bf16[2048,384]{1,0:T(8,128)(2,1)S(1)} %bitcast.32), custom_call_target="tpu_custom_call" | custom-call | flops 20000000000 | bytes 8388608 | tf_op jit(solution)/shard_map/gram/pallas_call | solution.py:186
  159.8 0.1 pad_maximum_fusion
  160.0 1.4 convolution_convert_fusion
  161.4 97.5 %exchange.3.rows_ref = bf16[2048,512]{1,0:T(8,128)(2,1)S(1)} custom-call(bf16[2048,384]{1,0:T(8,128)(2,1)S(1)} %bitcast.33, bf16[384,512]{1,0:T(8,128)(2,1)S(1)} %gram.1.right, bf16[128,128]{1,0:T(8,128)(2,1)S(1)} %compare_convert_fusion.same), custom_call_target="tpu_custom_call" | custom-call | flops 60000002048 | bytes 8388608 | tf_op jit(solution)/shard_map/exchange/pallas_call | solution.py:423
  258.9 1.3 copy-done.3
  260.3 22.4 %hidden.1 = bf16[1024,384]{1,0:T(8,128)(2,1)} custom-call(bf16[2048,512]{1,0:T(8,128)(2,1)} %copy-done.3, bf16[2048,384]{1,0:T(8,128)(2,1)} %bitcast.30, bf16[2048,384]{1,0:T(8,128)(2,1)} %bitcast.38, bf16[1024,2048]{1,0:T(8,128)(2,1)} %all-gather.5.cloned.1.call-done.slots_hbm), custom_call_target="tpu_custom_call" | custom-call | flops 20000000000 | bytes 8388608 | tf_op jit(solution)/shard_map/hidden/pallas_call | solution.py:186
  (24 shorter events, 0.4 us)
Async XLA Ops:
  6.5 107.6 %all-gather.3.cloned.1.call-start = ((), (), s32[]{:S(2)}) async-start(), calls=%async_computation | async-start | bytes 1183744 | tf_op jit(solution)/shard_map/all_gather | solution.py:29
  8.8 251.5 %all-gather.5.cloned.1.call-start = ((), (), s32[]{:S(2)}) async-start(), calls=%async_computation.1 | async-start | bytes 5242880 | tf_op jit(solution)/shard_map/all_gather | solution.py:465
  9.7 1.4 copy-start
  11.1 1.0 copy-start.2
  112.7 1.3 copy-start.4
  117.5 16.0 %copy-start.1 = (bf16[1,2048,384]{2,1,0:T(8,128)(2,1)S(1)}, bf16[1,2048,384]{2,1,0:T(8,128)(2,1)}, u32[]{:S(2)}) copy-start(bf16[1,2048,384]{2,1,0:T(8,128)(2,1)} %param.10) | copy-start | bytes 4718596
  117.6 5.7 %collective-permute-start = (bf16[4,32,2048]{2,1,0:T(8,128)(2,1)S(1)}, bf16[4,32,2048]{2,1,0:T(8,128)(2,1)S(1)}, u32[]{:S(2)}, u32[]{:S(2)}) collective-permute-start(bf16[4,32,2048]{2,1,0:T(8,128)(2,1)S(1)} %get-tuple-element.31), channel_id=1, source_target_pairs={{0,4},{4,0},{8,12},{12,8},{16,20},{20,16},{24,28},{28,24},{32,36},... | collective-permute-start | bytes 1572872 | tf_op jit(solution)/shard_map/ppermute | solution.py:63
  121.8 11.7 %copy-start.5 = (bf16[2048,512]{1,0:T(8,128)(2,1)S(1)}, bf16[2048,512]{1,0:T(8,128)(2,1)}, u32[]{:S(2)}) copy-start(bf16[2048,512]{1,0:T(8,128)(2,1)} %copy-done.4) | copy-start | bytes 6291460
  123.4 36.4 %collective-permute-start.3 = (bf16[2,32,2048]{2,1,0:T(8,128)(2,1)S(1)}, bf16[2,32,2048]{2,1,0:T(8,128)(2,1)S(1)}, u32[]{:S(2)}, u32[]{:S(2)}) collective-permute-start(bf16[2,32,2048]{2,1,0:T(8,128)(2,1)S(1)} %get-tuple-element.27), channel_id=1, source_target_pairs={{0,24},{4,28},{8,0},{12,4},{16,8},{20,12},{24,16},{28,20},{32,56},... | collective-permute-start | bytes 786440 | tf_op jit(solution)/shard_map/ppermute | solution.py:67
  128.5 31.4 %collective-permute-start.1 = (bf16[2,32,2048]{2,1,0:T(8,128)(2,1)S(1)}, bf16[2,32,2048]{2,1,0:T(8,128)(2,1)S(1)}, u32[]{:S(2)}, u32[]{:S(2)}) collective-permute-start(bf16[2,32,2048]{2,1,0:T(8,128)(2,1)S(1)} %get-tuple-element.29), channel_id=1, source_target_pairs={{0,8},{4,12},{8,16},{12,20},{16,24},{20,28},{24,0},{28,4},{32,40},... | collective-permute-start | bytes 786440 | tf_op jit(solution)/shard_map/ppermute | solution.py:67
  130.4 29.4 %collective-permute-start.2 = (bf16[2,32,2048]{2,1,0:T(8,128)(2,1)S(1)}, bf16[2,32,2048]{2,1,0:T(8,128)(2,1)S(1)}, u32[]{:S(2)}, u32[]{:S(2)}) collective-permute-start(bf16[2,32,2048]{2,1,0:T(8,128)(2,1)S(1)} %get-tuple-element.30), channel_id=1, source_target_pairs={{0,16},{4,20},{8,24},{12,28},{16,0},{20,4},{24,8},{28,12},{32,48},... | collective-permute-start | bytes 786440 | tf_op jit(solution)/shard_map/ppermute | solution.py:67
  258.9 1.4 copy-start.3
Sparse Core Ops, SparseCore 0:
  9.4 93.7 all-gather.2
  161.6 66.9 all-gather.4
